TPU v7x, 32 devices: a whole 2x2x4 slice. The times are simulated.
32 devices in a mesh: gx: 8 (over z, x), gy: 4 (over y, core).
Axes of the slice: x: 2, y: 2, z: 4, core: 2. Of those that a mesh axis runs over, the one named last changes fastest.
Arguments:
- positions: float32 [8, 4, 3, 128], P('gx', 'gy'), may hold values from 0 to 29
- species: int32 [8, 4, 128], P('gx', 'gy'), may hold values from 0 to 4
- senders: int32 [8, 4, 3, 128], P('gx', 'gy'), may hold values from 0 to 639, as said below
- counts: int32 [8, 4, 128], P('gx', 'gy'), may hold values from 1 to 3, as said below
- owners: int32 [8, 4, 3, 128], P('gx', 'gy'), may hold values 0 or 1
- send_list: int32 [8, 4, 64], P('gx', 'gy'), may hold values from 0 to 127, as said below
- embedding: float32 [128, 5], replicated, may hold values from -6 to 6
- radial_in_one: float32 [64, 8], replicated, may hold values from -2 to 2
- radial_mid_one: float32 [64, 64], replicated, may hold values from -0.75 to 0.75
- radial_out_one: float32 [384, 64], replicated, may hold values from -0.75 to 0.75
- mixing: float32 [3, 128, 128], replicated, may hold values from -0.5 to 0.5
- square_mix: float32 [128, 128], replicated, may hold values from -0.5 to 0.5
- readout_one: float32 [128], replicated, may hold values from -0.5 to 0.5
- radial_in_two: float32 [64, 8], replicated, may hold values from -2 to 2
- radial_mid_two: float32 [64, 64], replicated, may hold values from -0.75 to 0.75
- radial_out_two: float32 [384, 64], replicated, may hold values from -0.75 to 0.75
- mix_two: float32 [128, 128], replicated, may hold values from -0.5 to 0.5
- read_hidden: float32 [16, 128], replicated, may hold values from -0.5 to 0.5
- read_out: float32 [16], replicated, may hold values from -1.5 to 1.5
Outputs:
- forces: float32 [8, 4, 3, 128], P('gx', 'gy')
- energies: float32 [8, 4, 128], P('gx', 'gy')
Inputs may be any that keep to these rules, and one draw needn't show every extreme that they name: `counts`: every atom has at least one live slot, and some atom of every domain has all 3 slots live. `send_list`: each domain's list holds 64 distinct atoms of that domain. `senders`: an atom's slots name distinct atoms other than itself. Atom n of a domain sits at lattice site ((n // 2) // 8, (n // 2) % 8, n % 2); a ghost taken from the domain at offset (i - 1, j - 1) sits at its own site in that domain plus ((i - 1) * 8, (j - 1) * 8, 0). The site of every atom that a slot names differs from the site of the slot's atom by at most one along each of the three dimensions.
All inputs are finite; a program needn't handle non-finite values. No bound on the sum of `owners` on one device may be relied on, other than what follows from the above.
Results may differ from a plain program's by a relative error of at most 0.0003.
Values sent between devices are 32-bit elements; how exact they have to be, the bound alone decides.
A program may use at most 64 MiB of HBM per device.

v0:
```python
import math

import jax
import jax.numpy as jnp
from jax import lax
from jax.sharding import PartitionSpec as P

SIDE = 8


precise = lax.Precision.HIGHEST
spacing = 1.75
cutoff = 5.0
soften = 0.25
pair_strength = 2.0


def from_behind(value, axis, steps):
    count = lax.axis_size(axis)
    pairs = [(source, (source + steps) % count) for source in range(count)]
    return lax.ppermute(value, axis, pairs)


def extended(cells, sides, width):
    for axis, dim in sides:
        count = lax.axis_size(axis)
        head = lax.slice_in_dim(cells, 0, width, axis=dim)
        tail = lax.slice_in_dim(cells, cells.shape[dim] - width, cells.shape[dim], axis=dim)
        cells = jnp.concatenate(
            [
                lax.ppermute(tail, axis, [(i, (i + 1) % count) for i in range(count)]),
                cells,
                lax.ppermute(head, axis, [((i + 1) % count, i) for i in range(count)]),
            ],
            axis=dim,
        )
    return cells


def product(left_side, right_side):
    return jnp.dot(left_side, right_side, precision=precise, preferred_element_type=jnp.float32)


def harmonics(direction):
    along_x = direction[0]
    along_y = direction[1]
    along_z = direction[2]
    root_three = math.sqrt(3.0)
    root_five = math.sqrt(5.0)
    root_fifteen = math.sqrt(15.0)
    return jnp.stack(
        [
            jnp.ones_like(along_x),
            root_three * along_x,
            root_three * along_y,
            root_three * along_z,
            root_fifteen * along_x * along_y,
            root_fifteen * along_y * along_z,
            0.5 * root_five * (2.0 * along_z * along_z - along_x * along_x - along_y * along_y),
            root_fifteen * along_x * along_z,
            0.5 * root_fifteen * (along_x * along_x - along_y * along_y),
        ]
    )


def geometry(places, ghost_places, table_index, basis_count):
    places_all = jnp.concatenate([places, ghost_places], axis=1)
    repeats = table_index.shape[0] // places.shape[1]
    displace = places_all[:, table_index] - jnp.tile(places, (1, repeats))
    radius = jnp.sqrt(jnp.sum(displace * displace, axis=0) + soften)
    direction = displace / radius
    scaled_radius = jnp.minimum(radius / cutoff, 1.0)
    envelope = 1.0 - 28.0 * scaled_radius**6 + 48.0 * scaled_radius**7 - 21.0 * scaled_radius**8
    orders = jnp.arange(1, basis_count + 1).astype(jnp.float32)[:, None]
    radial_basis = (
        math.sqrt(2.0 / cutoff) * jnp.sin(orders * math.pi * scaled_radius) / radius * envelope
    )
    return (harmonics(direction), radial_basis, envelope, radius)


def radial(radial_basis, weight_in, weight_mid, weight_out):
    hidden = jax.nn.silu(product(weight_in, radial_basis))
    hidden = jax.nn.silu(product(weight_mid, hidden))
    return product(weight_out, hidden)


def flat_index(senders, atom_count, bound_count):
    ghost_slot = senders - atom_count
    blocks_of = ghost_slot // bound_count
    blocks_of = blocks_of + (blocks_of >= 4).astype(jnp.int32)
    spot = atom_count + blocks_of * bound_count + ghost_slot % bound_count
    return jnp.where(senders < atom_count, senders, spot).reshape(-1)


def live_slots(counts, slot_count):
    return (jnp.arange(slot_count)[:, None] < counts[None, :]).astype(jnp.float32).reshape(-1)


def ghost_shift(bound_count):
    blocks_of = jnp.arange(9 * bound_count) // bound_count
    side_length = spacing * SIDE
    shift_x = (blocks_of // 3 - 1).astype(jnp.float32) * side_length
    shift_y = (blocks_of % 3 - 1).astype(jnp.float32) * side_length
    return jnp.stack([shift_x, shift_y, jnp.zeros_like(shift_x)])


def lookup(embedding, element_codes):
    one_hot = (jnp.arange(embedding.shape[1])[:, None] == element_codes[None, :]).astype(
        jnp.float32
    )
    return product(embedding, one_hot)


def blocks_to_table(arrived):
    rows_each = arrived.shape[2]
    stacked = arrived.reshape(9, rows_each, arrived.shape[3])
    return jnp.moveaxis(stacked, 0, 1).reshape(rows_each, -1)


def layer_one(
    places,
    ghost_places,
    embedded,
    ghost_embedded,
    table_index,
    live_mask,
    owner_mask,
    weight_in,
    weight_mid,
    weight_out,
    mixing,
    square_mix,
    readout_one,
):
    shapes, radial_basis, envelope, radius = geometry(
        places, ghost_places, table_index, weight_in.shape[1]
    )
    atom_count = places.shape[1]
    channels = embedded.shape[0]
    slot_count = table_index.shape[0] // atom_count
    edge_weight = radial(radial_basis, weight_in, weight_mid, weight_out).reshape(3, channels, -1)
    sender_rows = jnp.concatenate([embedded, ghost_embedded], axis=1)[:, table_index]
    carried = (edge_weight * (sender_rows * live_mask)[None]).reshape(
        3, channels, slot_count, atom_count
    )
    shaped = shapes.reshape(9, slot_count, atom_count)
    scalar_part = jnp.einsum("cna,na->ca", carried[0], shaped[0], precision=precise)[None]
    vector_part = jnp.einsum("cna,kna->kca", carried[1], shaped[1:4], precision=precise)
    tensor_part = jnp.einsum("cna,kna->kca", carried[2], shaped[4:9], precision=precise)
    moments = jnp.concatenate([scalar_part, vector_part, tensor_part], 0) / slot_count
    squares = jnp.sum(moments * moments, axis=0)
    scalar_feature = product(mixing[0], moments[0]) + product(square_mix, squares) + embedded
    vectors = jnp.einsum("ij,kja->kia", mixing[1], moments[1:4], precision=precise)
    tensors = jnp.einsum("ij,kja->kia", mixing[2], moments[4:9], precision=precise)
    features = jnp.concatenate([scalar_feature[None], vectors, tensors], 0).reshape(
        9 * channels, atom_count
    )
    pair_energy = (
        (owner_mask * live_mask * pair_strength * jnp.exp(-radius) * envelope)
        .reshape(slot_count, atom_count)
        .sum(0)
    )
    energy = product(readout_one, scalar_feature) + pair_energy
    return (features, energy)


def layer_two(
    places,
    ghost_places,
    features,
    ghost_features,
    table_index,
    live_mask,
    weight_in,
    weight_mid,
    weight_out,
    mix_two,
    read_hidden,
    read_out,
):
    shapes, radial_basis, envelope, radius = geometry(
        places, ghost_places, table_index, weight_in.shape[1]
    )
    atom_count = places.shape[1]
    channels = mix_two.shape[0]
    slot_count = table_index.shape[0] // atom_count
    edge_weight = radial(radial_basis, weight_in, weight_mid, weight_out).reshape(3, channels, -1)
    sender_rows = jnp.concatenate([features, ghost_features], axis=1)[:, table_index].reshape(
        9, channels, -1
    )
    projected = sender_rows * shapes[:, None, :]
    scalar = (
        edge_weight[0] * projected[0]
        + edge_weight[1] * jnp.sum(projected[1:4], 0)
        + edge_weight[2] * jnp.sum(projected[4:9], 0)
    ) * live_mask
    gathered = scalar.reshape(channels, slot_count, atom_count).sum(1) / slot_count
    refined = product(mix_two, gathered) + features[:channels]
    return product(read_out, jax.nn.silu(product(read_hidden, refined)))


def send_back(ghost_grad, bound_count):
    rows_each = ghost_grad.shape[0]
    pieces = ghost_grad.reshape(rows_each, 3, 3, bound_count)
    from_lower = from_behind(pieces[:, 2], "gx", 1)
    from_upper = from_behind(pieces[:, 0], "gx", -1)
    merged = pieces[:, 1] + from_lower + from_upper
    from_below = from_behind(merged[:, 2], "gy", 1)
    from_above = from_behind(merged[:, 0], "gy", -1)
    return merged[:, 1] + from_below + from_above


def local(
    positions,
    species,
    senders,
    counts,
    owners,
    send_list,
    embedding,
    radial_in_one,
    radial_mid_one,
    radial_out_one,
    mixing,
    square_mix,
    readout_one,
    radial_in_two,
    radial_mid_two,
    radial_out_two,
    mix_two,
    read_hidden,
    read_out,
):
    places = positions[0, 0]
    species_here = species[0, 0]
    outgoing = send_list[0, 0]
    atom_count = places.shape[1]
    bound_count = outgoing.shape[0]
    table_index = flat_index(senders[0, 0], atom_count, bound_count)
    live_mask = live_slots(counts[0, 0], senders.shape[2])
    owner_mask = owners[0, 0].astype(jnp.float32).reshape(-1)
    embedded = lookup(embedding, species_here)
    bound_places = places[:, outgoing]
    code_rows = species_here[outgoing].astype(jnp.float32)[None]
    outbound = jnp.concatenate([bound_places, code_rows], 0)
    arrived = extended(outbound[None, None], (("gx", 0), ("gy", 1)), 1)
    spread = blocks_to_table(arrived)
    ghost_places = spread[:3]
    ghost_embedded = lookup(embedding, spread[3].astype(jnp.int32))
    ghost_places = ghost_places + ghost_shift(bound_count)

    def first_layer(place_arg, ghost_arg):
        return layer_one(
            place_arg,
            ghost_arg,
            embedded,
            ghost_embedded,
            table_index,
            live_mask,
            owner_mask,
            radial_in_one,
            radial_mid_one,
            radial_out_one,
            mixing,
            square_mix,
            readout_one,
        )

    outputs_one, pullback_one = jax.vjp(first_layer, places, ghost_places)
    features, energy_one = outputs_one
    outbound_two = features[:, outgoing][None, None]
    arrived_two = extended(outbound_two, (("gx", 0), ("gy", 1)), 1)
    ghost_features = blocks_to_table(arrived_two)

    def second_layer(place_arg, ghost_arg, feature_arg, ghost_feature_arg):
        return layer_two(
            place_arg,
            ghost_arg,
            feature_arg,
            ghost_feature_arg,
            table_index,
            live_mask,
            radial_in_two,
            radial_mid_two,
            radial_out_two,
            mix_two,
            read_hidden,
            read_out,
        )

    energy_two, pullback_two = jax.vjp(second_layer, places, ghost_places, features, ghost_features)
    grad_places, grad_ghosts, grad_features, grad_ghost_features = pullback_two(
        jnp.ones_like(energy_two)
    )
    returned = send_back(jnp.concatenate([grad_ghost_features, grad_ghosts], 0), bound_count)
    feature_back = returned[:-3]
    place_back_two = returned[-3:]
    grad_features = grad_features.at[:, outgoing].add(feature_back)
    grad_first, grad_ghost_first = pullback_one((grad_features, jnp.ones_like(energy_one)))
    place_back = send_back(grad_ghost_first, bound_count) + place_back_two
    grad_total = (grad_places + grad_first).at[:, outgoing].add(place_back)
    return ((-grad_total)[None, None], (energy_one + energy_two)[None, None])


def solution(mesh):
    placed = (
        P("gx", "gy", None, None),
        P("gx", "gy", None),
        P("gx", "gy", None, None),
        P("gx", "gy", None),
        P("gx", "gy", None, None),
        P("gx", "gy", None),
        P(),
        P(),
        P(),
        P(),
        P(),
        P(),
        P(),
        P(),
        P(),
        P(),
        P(),
        P(),
        P(),
    )
    return jax.shard_map(
        local,
        mesh=mesh,
        in_specs=placed,
        out_specs=(P("gx", "gy", None, None), P("gx", "gy", None)),
        check_vma=False,
    )
```

profile of v0, /device:TPU:1, one launch (start us, length us, event | category | flops | bytes accessed | tf_op | source)
XLA Modules:
  0.0 201.5 jit_solution(15553582411567846613)
XLA Ops:
  2.1 1.4 gather_fusion.1
  4.3 5.1 %collective-permute-start.1 = (f32[1,1,4,64]{3,2,1,0:T(4,128)S(1)}, f32[1,1,4,64]{3,2,1,0:T(4,128)S(1)}, u32[]{:S(2)}, u32[]{:S(2)}) collective-permute-start(f32[1,1,4,64]{3,2,1,0:T(4,128)S(1)} %maximum_bitcast_fusion), channel_id=1, source_target_pairs={{4,0},{8,4},{12,8},{16,12},{20,16},{24,20},{28,24},{0,28},{5,1},{9... | collective-permute-start | bytes 3080 | tf_op jit(solution)/shard_map/ppermute | solution.py:33
  11.9 2.7 %collective-permute-done = f32[1,1,4,64]{3,2,1,0:T(4,128)S(1)} collective-permute-done((f32[1,1,4,64]{3,2,1,0:T(4,128)S(1)}, f32[1,1,4,64]{3,2,1,0:T(4,128)S(1)}, u32[]{:S(2)}, u32[]{:S(2)}) %collective-permute-start) | collective-permute-done | bytes 1056 | tf_op jit(solution)/shard_map/ppermute | solution.py:31
  14.6 2.1 %collective-permute-start.3 = (f32[3,1,4,64]{3,2,1,0:T(4,128)S(1)}, f32[3,1,4,64]{3,2,1,0:T(4,128)S(1)}, u32[]{:S(2)}, u32[]{:S(2)}) collective-permute-start(f32[3,1,4,64]{3,2,1,0:T(4,128)S(1)} %pad_maximum_fusion.9), channel_id=1, source_target_pairs={{1,0},{2,1},{3,2},{0,3},{5,4},{6,5},{7,6},{4,7},{9,8},{10,9},{11,1... | collective-permute-start | bytes 9224 | tf_op jit(solution)/shard_map/ppermute | solution.py:33
  16.7 1.2 collective-permute-start.2
  17.9 1.5 collective-permute-done.3
  19.7 1.1 convolution_bitcast_fusion.3
  21.1 1.1 gather_fusion.3
  22.2 1.1 gather_fusion.2
  28.1 1.2 convolution_bitcast_fusion.6
  29.4 1.2 convolution_bitcast_fusion.1
  35.2 1.1 collective-permute-start.4
  36.3 13.1 %collective-permute-done.5 = f32[1,1,1152,64]{2,3,1,0:T(8,128)S(1)} collective-permute-done((f32[1,1,1152,64]{2,3,1,0:T(8,128)S(1)}, f32[1,1,1152,64]{2,3,1,0:T(8,128)S(1)}, u32[]{:S(2)}, u32[]{:S(2)}) %collective-permute-start.5) | collective-permute-done | bytes 294944 | tf_op jit(solution)/shard_map/ppermute | solution.py:33
  49.4 1.3 collective-permute-start.7
  51.2 1.2 stack.11
  53.1 1.5 convolution_bitcast_fusion
  54.7 16.4 %collective-permute-done.7 = f32[3,1,1152,64]{2,3,1,0:T(8,128)S(1)} collective-permute-done((f32[3,1,1152,64]{2,3,1,0:T(8,128)S(1)}, f32[3,1,1152,64]{2,3,1,0:T(8,128)S(1)}, u32[]{:S(2)}, u32[]{:S(2)}) %collective-permute-start.7) | collective-permute-done | bytes 884768 | tf_op jit(solution)/shard_map/ppermute | solution.py:33
  71.1 1.3 pad_maximum_fusion.2
  72.7 2.8 %gather_fusion.5 = f32[384,1152]{1,0:T(8,128)} fusion(f32[1152,704]{0,1:T(8,128)S(1)} %pad_maximum_fusion, s32[1024]{0:T(1024)} %copy-done.50), kind=kCustom, calls=%fused_computation.5 | custom fusion | bytes 3540480 | tf_op jit(solution)/shard_map/jvp()/gather | solution.py:188
  75.5 2.2 %copy.489 = f32[1152,384]{1,0:T(8,128)S(1)} copy(f32[1152,384]{0,1:T(8,128)} %bitcast.397) | data formatting | bytes 3538944 | tf_op jit(solution)/shard_map/jvp()/gather | solution.py:188
  78.0 1.1 copy-done.4
  79.9 1.1 copy.490
  82.3 1.1 fusion.120
  86.2 1.5 multiply_reduce_fusion
  91.7 1.9 copy.496
  94.7 2.1 %scatter_custom_fusion = f32[3,704]{0,1:T(8,128)S(1)} fusion(s32[384]{0:T(512)} %copy-done.57, f32[384,3]{1,0:T(8,128)S(1)} %copy.494, f32[]{:T(128)} %constant.112.clone.1), kind=kCustom, calls=%fused_computation.116 | custom fusion | flops 1152 | bytes 8960 | tf_op jit(solution)/shard_map/transpose(jvp())/scatter-add | solution.py:69
  98.3 5.9 %scatter_custom_fusion.1 = f32[1152,704]{0,1:T(8,128)S(1)} fusion(s32[384]{0:T(512)} %copy-done.57, f32[1152,384]{0,1:T(8,128)} %copy.496, f32[]{:T(128)} %constant.112.clone.1), kind=kCustom, calls=%fused_computation.14 | custom fusion | flops 442368 | bytes 5014016 | tf_op jit(solution)/shard_map/transpose(jvp())/scatter-add | solution.py:188
  105.4 1.6 copy-done.3
  107.0 1.5 slice_bitcast_fusion.1
  108.5 4.2 %collective-permute-start.9 = (f32[1155,3,64]{0,2,1:T(8,128)}, f32[1155,3,64]{0,2,1:T(8,128)}, u32[]{:S(2)}, u32[]{:S(2)}) collective-permute-start(f32[1155,3,64]{0,2,1:T(8,128)} %get-tuple-element.31), channel_id=1, source_target_pairs={{0,28},{4,0},{8,4},{12,8},{16,12},{20,16},{24,20},{28,24},{1,29},{... | collective-permute-start | bytes 2661128 | tf_op jit(solution)/shard_map/ppermute | solution.py:21
  113.7 1.7 copy.525
  116.2 1.6 fusion.11
  117.8 33.3 %collective-permute-done.8 = f32[1155,3,64]{0,2,1:T(8,128)} collective-permute-done((f32[1155,3,64]{0,2,1:T(8,128)}, f32[1155,3,64]{0,2,1:T(8,128)}, u32[]{:S(2)}, u32[]{:S(2)}) %collective-permute-start.8) | collective-permute-done | bytes 887072 | tf_op jit(solution)/shard_map/ppermute | solution.py:21
  151.9 1.9 fusion.14
  153.9 3.3 %collective-permute-start.10 = (f32[1155,64]{0,1:T(8,128)S(1)}, f32[1155,64]{0,1:T(8,128)S(1)}, u32[]{:S(2)}, u32[]{:S(2)}) collective-permute-start(f32[1155,64]{0,1:T(8,128)S(1)} %get-tuple-element.34), channel_id=1, source_target_pairs={{0,1},{1,2},{2,3},{3,0},{4,5},{5,6},{6,7},{7,4},{8,9},{9,10},{10,1... | collective-permute-start | bytes 887048 | tf_op jit(solution)/shard_map/ppermute | solution.py:21
  158.1 5.9 %collective-permute-done.10 = f32[1155,64]{0,1:T(8,128)S(1)} collective-permute-done((f32[1155,64]{0,1:T(8,128)S(1)}, f32[1155,64]{0,1:T(8,128)S(1)}, u32[]{:S(2)}, u32[]{:S(2)}) %collective-permute-start.10) | collective-permute-done | bytes 295712 | tf_op jit(solution)/shard_map/ppermute | solution.py:21
  164.0 1.4 collective-permute-done.11
  165.4 3.1 %scatter_custom_fusion.2 = f32[1152,128]{0,1:T(8,128)} fusion(f32[1152,128]{0,1:T(8,128)} %slice_add_fusion, s32[64]{0:T(128)} %copy-done.70, f32[1155,64]{0,1:T(8,128)S(1)} %fusion.19), kind=kCustom, calls=%fused_computation.88 | custom fusion | flops 73728 | bytes 884736 | tf_op jit(solution)/shard_map/scatter-add | solution.py:298
  168.6 1.7 fusion.4
  170.3 1.7 fusion.74
  173.0 1.1 split.58
  175.8 1.5 fusion.12
  185.2 2.1 %scatter_custom_fusion.3 = f32[3,704]{0,1:T(8,128)S(1)} fusion(s32[384]{0:T(512)} %copy-done.57, f32[384,3]{1,0:T(8,128)S(1)} %copy.512, f32[]{:T(128)} %constant.112.clone.1), kind=kCustom, calls=%fused_computation.114 | custom fusion | flops 1152 | bytes 8960 | tf_op jit(solution)/shard_map/transpose(jvp())/scatter-add | solution.py:69
  187.3 4.1 %collective-permute-start.13 = (f32[3,3,64]{0,2,1:T(8,128)S(1)}, f32[3,3,64]{0,2,1:T(8,128)S(1)}, u32[]{:S(2)}, u32[]{:S(2)}) collective-permute-start(f32[3,3,64]{0,2,1:T(8,128)S(1)} %get-tuple-element.45), channel_id=1, source_target_pairs={{0,28},{4,0},{8,4},{12,8},{16,12},{20,16},{24,20},{28,24},{1,29},{... | collective-permute-start | bytes 6920 | tf_op jit(solution)/shard_map/ppermute | solution.py:21
  192.4 2.3 %collective-permute-done.12 = f32[3,3,64]{0,2,1:T(8,128)S(1)} collective-permute-done((f32[3,3,64]{0,2,1:T(8,128)S(1)}, f32[3,3,64]{0,2,1:T(8,128)S(1)}, u32[]{:S(2)}, u32[]{:S(2)}) %collective-permute-start.12) | collective-permute-done | bytes 2336 | tf_op jit(solution)/shard_map/ppermute | solution.py:21
  194.7 1.8 collective-permute-start.14
  197.5 2.3 %collective-permute-done.15 = f32[3,64]{0,1:T(8,128)S(1)} collective-permute-done((f32[3,64]{0,1:T(8,128)S(1)}, f32[3,64]{0,1:T(8,128)S(1)}, u32[]{:S(2)}, u32[]{:S(2)}) %collective-permute-start.15) | collective-permute-done | bytes 800 | tf_op jit(solution)/shard_map/ppermute | solution.py:21
  199.8 1.1 scatter_custom_fusion.4
  (331 shorter events, 44.5 us)
Async XLA Ops:
  0.6 52.5 %copy-start = (f32[384,64]{0,1:T(8,128)S(1)}, f32[384,64]{0,1:T(8,128)}, u32[]{:S(2)}) copy-start(f32[384,64]{0,1:T(8,128)} %param.34) | copy-start | bytes 294916
  0.6 24.0 %copy-start.76 = (f32[64,8]{0,1:T(8,128)S(1)}, f32[64,8]{0,1:T(8,128)}, u32[]{:S(2)}) copy-start(f32[64,8]{0,1:T(8,128)} %param.26) | copy-start | bytes 6148
  0.7 24.3 %copy-start.72 = (f32[64,64]{1,0:T(8,128)S(1)}, f32[64,64]{1,0:T(8,128)}, u32[]{:S(2)}) copy-start(f32[64,64]{1,0:T(8,128)} %param.27) | copy-start | bytes 49156
  1.4 18.1 %copy-start.70 = (s32[64]{0:T(128)}, s32[64]{0:T(128)S(1)}, u32[]{:S(2)}) copy-start(s32[64]{0:T(128)S(1)} %fusion.175) | copy-start | bytes 772
  3.5 21.8 %copy-start.31 = (f32[384,64]{0,1:T(8,128)S(1)}, f32[384,64]{0,1:T(8,128)}, u32[]{:S(2)}) copy-start(f32[384,64]{0,1:T(8,128)} %param.28) | copy-start | bytes 294916
  4.3 7.6 %collective-permute-start.1 = (f32[1,1,4,64]{3,2,1,0:T(4,128)S(1)}, f32[1,1,4,64]{3,2,1,0:T(4,128)S(1)}, u32[]{:S(2)}, u32[]{:S(2)}) collective-permute-start(f32[1,1,4,64]{3,2,1,0:T(4,128)S(1)} %maximum_bitcast_fusion), channel_id=1, source_target_pairs={{4,0},{8,4},{12,8},{16,12},{20,16},{24,20},{28,24},{0,28},{5,1},{9... | collective-permute-start | bytes 3080 | tf_op jit(solution)/shard_map/ppermute | solution.py:33
  9.4 5.1 %collective-permute-start = (f32[1,1,4,64]{3,2,1,0:T(4,128)S(1)}, f32[1,1,4,64]{3,2,1,0:T(4,128)S(1)}, u32[]{:S(2)}, u32[]{:S(2)}) collective-permute-start(f32[1,1,4,64]{3,2,1,0:T(4,128)S(1)} %maximum_bitcast_fusion), channel_id=1, source_target_pairs={{0,4},{4,8},{8,12},{12,16},{16,20},{20,24},{24,28},{28,0},{1,5},{5... | collective-permute-start | bytes 3080 | tf_op jit(solution)/shard_map/ppermute | solution.py:31
  10.2 9.3 %copy-start.57 = (s32[384]{0:T(512)}, s32[384]{0:T(512)S(1)}, u32[]{:S(2)}) copy-start(s32[384]{0:T(512)S(1)} %fusion.154) | copy-start | bytes 4612
  10.8 15.3 %copy-start.40 = (f32[384]{0:T(512)}, f32[384]{0:T(512)S(1)}, u32[]{:S(2)}) copy-start(f32[384]{0:T(512)S(1)} %fusion.150) | copy-start | bytes 4612
  11.8 12.4 %copy-start.50 = (s32[1024]{0:T(1024)}, s32[1024]{0:T(1024)S(1)}, u32[]{:S(2)}) copy-start(s32[1024]{0:T(1024)S(1)} %pad_clamp_fusion) | copy-start | bytes 12292
  14.6 4.9 %collective-permute-start.3 = (f32[3,1,4,64]{3,2,1,0:T(4,128)S(1)}, f32[3,1,4,64]{3,2,1,0:T(4,128)S(1)}, u32[]{:S(2)}, u32[]{:S(2)}) collective-permute-start(f32[3,1,4,64]{3,2,1,0:T(4,128)S(1)} %pad_maximum_fusion.9), channel_id=1, source_target_pairs={{1,0},{2,1},{3,2},{0,3},{5,4},{6,5},{7,6},{4,7},{9,8},{10,9},{11,1... | collective-permute-start | bytes 9224 | tf_op jit(solution)/shard_map/ppermute | solution.py:33
  16.7 2.8 %collective-permute-start.2 = (f32[3,1,4,64]{3,2,1,0:T(4,128)S(1)}, f32[3,1,4,64]{3,2,1,0:T(4,128)S(1)}, u32[]{:S(2)}, u32[]{:S(2)}) collective-permute-start(f32[3,1,4,64]{3,2,1,0:T(4,128)S(1)} %pad_maximum_fusion.9), channel_id=1, source_target_pairs={{0,1},{1,2},{2,3},{3,0},{4,5},{5,6},{6,7},{7,4},{8,9},{9,10},{10,1... | collective-permute-start | bytes 9224 | tf_op jit(solution)/shard_map/ppermute | solution.py:31
  17.9 34.6 %copy-start.82 = (f32[8]{0:T(128)}, f32[8]{0:T(128)S(1)}, u32[]{:S(2)}) copy-start(f32[8]{0:T(128)S(1)} %convert_multiply_fusion.1) | copy-start | bytes 100
  24.1 28.4 %copy-start.47 = (f32[384]{0:T(512)}, f32[384]{0:T(512)S(1)}, u32[]{:S(2)}) copy-start(f32[384]{0:T(512)S(1)} %get-tuple-element.64) | copy-start | bytes 4612
  24.1 28.4 %copy-start.61 = (f32[384]{0:T(512)}, f32[384]{0:T(512)S(1)}, u32[]{:S(2)}) copy-start(f32[384]{0:T(512)S(1)} %get-tuple-element.62) | copy-start | bytes 4612
  24.1 28.4 %copy-start.64 = (f32[384]{0:T(512)}, f32[384]{0:T(512)S(1)}, u32[]{:S(2)}) copy-start(f32[384]{0:T(512)S(1)} %get-tuple-element.63) | copy-start | bytes 4612
  24.4 5.0 %copy-start.17 = (f32[5,3,128]{0,1,2:T(4,128)}, f32[5,3,128]{0,1,2:T(4,128)S(1)}, u32[]{:S(2)}) copy-start(f32[5,3,128]{0,1,2:T(4,128)S(1)} %copy.480) | copy-start | bytes 23044
  28.1 4.1 %copy-start.27 = (f32[1,128,128]{1,0,2:T(1,128)}, f32[1,128,128]{1,0,2:T(1,128)S(1)}, u32[]{:S(2)}) copy-start(f32[1,128,128]{1,0,2:T(1,128)S(1)} %convolution_bitcast_fusion.18) | copy-start | bytes 196612
  28.1 4.1 %copy-start.25 = (f32[3,128,128]{2,1,0:T(8,128)S(1)}, f32[3,128,128]{2,1,0:T(8,128)}, u32[]{:S(2)}) copy-start(f32[3,128,128]{2,1,0:T(8,128)} %param.29) | copy-start | bytes 589828
  34.0 18.4 %copy-start.74 = (f32[64,8]{0,1:T(8,128)S(1)}, f32[64,8]{0,1:T(8,128)}, u32[]{:S(2)}) copy-start(f32[64,8]{0,1:T(8,128)} %param.32) | copy-start | bytes 6148
  34.1 18.8 %copy-start.71 = (f32[64,64]{1,0:T(8,128)S(1)}, f32[64,64]{1,0:T(8,128)}, u32[]{:S(2)}) copy-start(f32[64,64]{1,0:T(8,128)} %param.33) | copy-start | bytes 49156
  34.9 14.5 %collective-permute-start.5 = (f32[1,1,1152,64]{2,3,1,0:T(8,128)S(1)}, f32[1,1,1152,64]{2,3,1,0:T(8,128)S(1)}, u32[]{:S(2)}, u32[]{:S(2)}) collective-permute-start(f32[1,1,1152,64]{2,3,1,0:T(8,128)S(1)} %bitcast.399), channel_id=1, source_target_pairs={{4,0},{8,4},{12,8},{16,12},{20,16},{24,20},{28,24},{0,28},{5,1},{9... | collective-permute-start | bytes 884744 | tf_op jit(solution)/shard_map/ppermute | solution.py:33
  35.2 14.2 %collective-permute-start.4 = (f32[1,1,1152,64]{2,3,1,0:T(8,128)S(1)}, f32[1,1,1152,64]{2,3,1,0:T(8,128)S(1)}, u32[]{:S(2)}, u32[]{:S(2)}) collective-permute-start(f32[1,1,1152,64]{2,3,1,0:T(8,128)S(1)} %bitcast.400), channel_id=1, source_target_pairs={{0,4},{4,8},{8,12},{12,16},{16,20},{20,24},{24,28},{28,0},{1,5},{5... | collective-permute-start | bytes 884744 | tf_op jit(solution)/shard_map/ppermute | solution.py:31
  49.4 21.6 %collective-permute-start.7 = (f32[3,1,1152,64]{2,3,1,0:T(8,128)S(1)}, f32[3,1,1152,64]{2,3,1,0:T(8,128)S(1)}, u32[]{:S(2)}, u32[]{:S(2)}) collective-permute-start(f32[3,1,1152,64]{2,3,1,0:T(8,128)S(1)} %pad_maximum_fusion.4), channel_id=1, source_target_pairs={{1,0},{2,1},{3,2},{0,3},{5,4},{6,5},{7,6},{4,7},{9,8},{10,9},{11,1... | collective-permute-start | bytes 2654216 | tf_op jit(solution)/shard_map/ppermute | solution.py:33
  50.7 20.4 %collective-permute-start.6 = (f32[3,1,1152,64]{2,3,1,0:T(8,128)S(1)}, f32[3,1,1152,64]{2,3,1,0:T(8,128)}, u32[]{:S(2)}, u32[]{:S(2)}) collective-permute-start(f32[3,1,1152,64]{2,3,1,0:T(8,128)S(1)} %pad_maximum_fusion.4), channel_id=1, source_target_pairs={{0,1},{1,2},{2,3},{3,0},{4,5},{5,6},{6,7},{7,4},{8,9},{9,10},{10,1... | collective-permute-start | bytes 2654216 | tf_op jit(solution)/shard_map/ppermute | solution.py:31
  52.8 19.6 %copy-start.80 = (f32[64,384]{1,0:T(8,128)}, f32[64,384]{1,0:T(8,128)S(1)}, u32[]{:S(2)}) copy-start(f32[64,384]{1,0:T(8,128)S(1)} %convolution_bitcast_fusion.13) | copy-start | bytes 294916
  53.1 19.3 %copy-start.38 = (f32[64,384]{1,0:T(8,128)}, f32[64,384]{1,0:T(8,128)S(1)}, u32[]{:S(2)}) copy-start(f32[64,384]{1,0:T(8,128)S(1)} %convolution_bitcast_fusion.12) | copy-start | bytes 294916
  54.6 17.8 %copy-start.2 = (f32[1152,128]{0,1:T(8,128)S(1)}, f32[1152,128]{0,1:T(8,128)}, u32[]{:S(2)}) copy-start(f32[1152,128]{0,1:T(8,128)} %copy-done.1) | copy-start | bytes 1769476
  77.9 4.4 %copy-start.67 = (f32[16]{0:T(128)S(1)}, f32[16]{0:T(128)}, u32[]{:S(2)}) copy-start(f32[16]{0:T(128)} %param.37) | copy-start | bytes 196
  87.6 4.0 %copy-start.5 = (f32[9,128,384]{2,1,0:T(8,128)S(1)}, f32[9,128,384]{2,1,0:T(8,128)}, u32[]{:S(2)}) copy-start(f32[9,128,384]{2,1,0:T(8,128)} %get-tuple-element.33) | copy-start | bytes 5308420
  90.1 3.9 %copy-start.43 = (f32[384]{0:T(512)S(1)}, f32[384]{0:T(512)}, u32[]{:S(2)}) copy-start(f32[384]{0:T(512)} %copy-done.42) | copy-start | bytes 4612
  105.4 7.2 %copy-start.59 = (s32[1,1,3,128]{3,1,2,0:T(1,128)S(1)}, s32[1,1,3,128]{3,1,2,0:T(1,128)}, u32[]{:S(2)}) copy-start(s32[1,1,3,128]{3,1,2,0:T(1,128)} %param.23) | copy-start | bytes 4612
  108.5 42.7 %collective-permute-start.8 = (f32[1155,3,64]{0,2,1:T(8,128)}, f32[1155,3,64]{0,2,1:T(8,128)}, u32[]{:S(2)}, u32[]{:S(2)}) collective-permute-start(f32[1155,3,64]{0,2,1:T(8,128)} %get-tuple-element.30), channel_id=1, source_target_pairs={{0,4},{4,8},{8,12},{12,16},{16,20},{20,24},{24,28},{28,0},{1,5},{5... | collective-permute-start | bytes 2661128 | tf_op jit(solution)/shard_map/ppermute | solution.py:21
  108.5 43.5 %collective-permute-start.9 = (f32[1155,3,64]{0,2,1:T(8,128)}, f32[1155,3,64]{0,2,1:T(8,128)}, u32[]{:S(2)}, u32[]{:S(2)}) collective-permute-start(f32[1155,3,64]{0,2,1:T(8,128)} %get-tuple-element.31), channel_id=1, source_target_pairs={{0,28},{4,0},{8,4},{12,8},{16,12},{20,16},{24,20},{28,24},{1,29},{... | collective-permute-start | bytes 2661128 | tf_op jit(solution)/shard_map/ppermute | solution.py:21
  116.2 41.0 %copy-start.30 = (f32[128,128]{1,0:T(8,128)S(1)}, f32[128,128]{1,0:T(8,128)}, u32[]{:S(2)}) copy-start(f32[128,128]{1,0:T(8,128)} %copy-done.29) | copy-start | bytes 196612
  153.9 10.0 %collective-permute-start.10 = (f32[1155,64]{0,1:T(8,128)S(1)}, f32[1155,64]{0,1:T(8,128)S(1)}, u32[]{:S(2)}, u32[]{:S(2)}) collective-permute-start(f32[1155,64]{0,1:T(8,128)S(1)} %get-tuple-element.34), channel_id=1, source_target_pairs={{0,1},{1,2},{2,3},{3,0},{4,5},{5,6},{6,7},{7,4},{8,9},{9,10},{10,1... | collective-permute-start | bytes 887048 | tf_op jit(solution)/shard_map/ppermute | solution.py:21
  157.2 8.2 %collective-permute-start.11 = (f32[1155,64]{0,1:T(8,128)S(1)}, f32[1155,64]{0,1:T(8,128)S(1)}, u32[]{:S(2)}, u32[]{:S(2)}) collective-permute-start(f32[1155,64]{0,1:T(8,128)S(1)} %get-tuple-element.35), channel_id=1, source_target_pairs={{0,3},{1,0},{2,1},{3,2},{4,7},{5,4},{6,5},{7,6},{8,11},{9,8},{10,9... | collective-permute-start | bytes 887048 | tf_op jit(solution)/shard_map/ppermute | solution.py:21
  158.0 16.3 %copy-start.26 = (f32[3,128,128]{2,1,0:T(8,128)S(1)}, f32[3,128,128]{2,1,0:T(8,128)}, u32[]{:S(2)}) copy-start(f32[3,128,128]{2,1,0:T(8,128)} %param.29) | copy-start | bytes 589828
  177.3 4.1 %copy-start.12 = (f32[1,128,384]{1,2,0:T(8,128)S(1)}, f32[1,128,384]{1,2,0:T(8,128)}, u32[]{:S(2)}) copy-start(f32[1,128,384]{1,2,0:T(8,128)} %copy-done.11) | copy-start | bytes 589828
  183.6 7.9 %copy-start.46 = (f32[16,128]{1,0:T(8,128)S(1)}, f32[16,128]{1,0:T(8,128)}, u32[]{:S(2)}) copy-start(f32[16,128]{1,0:T(8,128)} %copy-done.45) | copy-start | bytes 24580
  183.6 7.9 %copy-start.68 = (f32[16]{0:T(128)S(1)}, f32[16]{0:T(128)}, u32[]{:S(2)}) copy-start(f32[16]{0:T(128)} %param.37) | copy-start | bytes 196
  183.6 7.9 %copy-start.69 = (f32[128]{0:T(128)S(1)}, f32[128]{0:T(128)}, u32[]{:S(2)}) copy-start(f32[128]{0:T(128)} %fusion.11) | copy-start | bytes 1540
  183.7 8.5 %copy-start.51 = (f32[3,384]{1,0:T(4,128)S(1)}, f32[3,384]{1,0:T(4,128)}, u32[]{:S(2)}) copy-start(f32[3,384]{1,0:T(4,128)} %get-tuple-element.24) | copy-start | bytes 13828
  183.7 8.5 %slice-start = ((f32[3,704]{0,1:T(8,128)}), f32[3,128]{0,1:T(8,128)S(1)}, s32[]{:S(2)}) async-start(f32[3,704]{0,1:T(8,128)} %copy-done.20), calls=%async_computation | async-start | bytes 131072 | tf_op jit(solution)/shard_map/transpose(jvp())/split | solution.py:67
  187.3 7.4 %collective-permute-start.12 = (f32[3,3,64]{0,2,1:T(8,128)S(1)}, f32[3,3,64]{0,2,1:T(8,128)S(1)}, u32[]{:S(2)}, u32[]{:S(2)}) collective-permute-start(f32[3,3,64]{0,2,1:T(8,128)S(1)} %get-tuple-element.44), channel_id=1, source_target_pairs={{0,4},{4,8},{8,12},{12,16},{16,20},{20,24},{24,28},{28,0},{1,5},{5... | collective-permute-start | bytes 6920 | tf_op jit(solution)/shard_map/ppermute | solution.py:21
  187.3 7.3 %collective-permute-start.13 = (f32[3,3,64]{0,2,1:T(8,128)S(1)}, f32[3,3,64]{0,2,1:T(8,128)S(1)}, u32[]{:S(2)}, u32[]{:S(2)}) collective-permute-start(f32[3,3,64]{0,2,1:T(8,128)S(1)} %get-tuple-element.45), channel_id=1, source_target_pairs={{0,28},{4,0},{8,4},{12,8},{16,12},{20,16},{24,20},{28,24},{1,29},{... | collective-permute-start | bytes 6920 | tf_op jit(solution)/shard_map/ppermute | solution.py:21
  194.7 2.8 %collective-permute-start.14 = (f32[3,64]{0,1:T(8,128)S(1)}, f32[3,64]{0,1:T(8,128)S(1)}, u32[]{:S(2)}, u32[]{:S(2)}) collective-permute-start(f32[3,64]{0,1:T(8,128)S(1)} %get-tuple-element.49), channel_id=1, source_target_pairs={{0,1},{1,2},{2,3},{3,0},{4,5},{5,6},{6,7},{7,4},{8,9},{9,10},{10,1... | collective-permute-start | bytes 2312 | tf_op jit(solution)/shard_map/ppermute | solution.py:21
  196.5 3.3 %collective-permute-start.15 = (f32[3,64]{0,1:T(8,128)S(1)}, f32[3,64]{0,1:T(8,128)S(1)}, u32[]{:S(2)}, u32[]{:S(2)}) collective-permute-start(f32[3,64]{0,1:T(8,128)S(1)} %get-tuple-element.50), channel_id=1, source_target_pairs={{0,3},{1,0},{2,1},{3,2},{4,7},{5,4},{6,5},{7,6},{8,11},{9,8},{10,9... | collective-permute-start | bytes 2312 | tf_op jit(solution)/shard_map/ppermute | solution.py:21
  (54 other events, 119.1 us)
where the time goes:
time: 203 us; the launch traced here: 202 us
  waiting for transfers between devices  80.6 us (40%)
  local copies, waits for them, and re-layouts  33.7 us (17%)
  other arithmetic  32.6 us (16%)
  matrix products  27 us (13%)
  starting transfers between devices  25.1 us (12%)
  between operations  2.5 us (1%)
    ppermute x8, waiting for transfers between devices, from_behind(): return lax.ppermute(value, axis, pairs)  46.9 us
    ppermute x4, waiting for transfers between devices, extended(): lax.ppermute(head, axis, [((i + 1) % count, i) for i in range(count)])  31 us
    dot_general x24, matrix products, product(): jnp.dot(left_side, right_side, precision=precise, preferred_element_type=...  16.9 us
    ppermute x8, starting transfers between devices, from_behind(): return lax.ppermute(value, axis, pairs)  13.4 us
    unnamed x174, local copies, waits for them, and re-layouts  9.83 us
    ppermute x4, starting transfers between devices, extended(): lax.ppermute(head, axis, [((i + 1) % count, i) for i in range(count)])  8.84 us
    scatter-add x1, other arithmetic, layer_two(): jnp.concatenate([features, ghost_features], axis=1)[:, table_index]  5.87 us
    gather x2, local copies, waits for them, and re-layouts, layer_two(): jnp.concatenate([features, ghost_features], axis=1)[:, table_index]  5.01 us
  transfers between devices with their start and end apart: 16, of which 11 were waited for; matrix products, arithmetic and copies ran while one was open for 6% of the time, Pallas kernels for 0%

commit v1 on v0

v1 whole, which is shorter than its diff:
```python
import functools
import math

import jax
import jax.numpy as jnp
from jax import lax
from jax.experimental import pallas as pl
from jax.experimental.pallas import tpu as pltpu
from jax.sharding import PartitionSpec as P

SIDE = 8
SPACING = 1.75
CUTOFF = 5.0
SOFTEN = 0.25
PAIR = 2.0
ROWS = 16
DEGREE = (0, 1, 1, 1, 2, 2, 2, 2, 2)
MEMBERS = ((0,), (1, 2, 3), (4, 5, 6, 7, 8))
F32 = jnp.float32
BF16 = jnp.bfloat16
NN = (((1,), (0,)), ((), ()))
TN = (((0,), (0,)), ((), ()))
NT = (((1,), (1,)), ((), ()))


def dot(a, b, dims=NN):
    return lax.dot_general(a, b, dims, preferred_element_type=F32)


def split(x):
    high = x.astype(BF16)
    return high, (x - high.astype(F32)).astype(BF16)


def split_three(x):
    high = x.astype(BF16)
    rest = x - high.astype(F32)
    return (high,) + split(rest)


def mm(a, b, dims=NN):
    return dot(a[0], b[0], dims) + (dot(a[0], b[1], dims) + dot(a[1], b[0], dims))


def pick(parts, one_hot, dims=NN):
    out = dot(parts[-1], one_hot, dims)
    for part in parts[-2::-1]:
        out = out + dot(part, one_hot, dims)
    return out


def floor_div(x, by):
    return jnp.floor((x + 0.5) * (1.0 / by))


def one_hot_rows(index, rows):
    ids = lax.broadcasted_iota(jnp.int32, (rows, index.shape[1]), 0).astype(F32)
    return jnp.where(ids == index, 1.0, 0.0).astype(BF16)


def by_domain(stacked, domain, rows):
    out = jnp.where(domain == 0.0, stacked[:rows], 0.0)
    for d in range(1, 9):
        out = out + jnp.where(domain == float(d), stacked[d * rows : (d + 1) * rows], 0.0)
    return out


def silu_pair(h):
    gate = jax.nn.sigmoid(h)
    return h * gate, gate * (1.0 + h * (1.0 - gate))


def radial(basis, w_in, w_mid, w_out):
    s1, g1 = silu_pair(mm(w_in, split(basis)))
    s2, g2 = silu_pair(mm(w_mid, split(s1)))
    return mm(w_out, split(s2)), g1, g2


def radial_back(g_out, w_in, w_mid, w_out, g1, g2):
    gh2 = mm(w_out, split(g_out), TN) * g2
    gh1 = mm(w_mid, split(gh2), TN) * g1
    return mm(w_in, split(gh1), TN)


def kernel(
    layers,
    pos_ref, spec_ref, send_ref, cnt_ref, own_ref, list_ref, emb_ref,
    wi1_ref, wm1_ref, wo1_ref, mix_ref, sqm_ref, ro1_ref,
    wi2_ref, wm2_ref, wo2_ref, mx2_ref, rh_ref, ro2_ref,
    force_ref, energy_ref,
    table, grads, back, send_a, recv_a, send_b, recv_b,
):
    atoms = pos_ref.shape[3]
    bound = list_ref.shape[2]
    slots = send_ref.shape[2]
    channels = emb_ref.shape[0]
    species = emb_ref.shape[1]
    nbasis = wi1_ref.shape[1]
    column = SIDE * layers
    wide = 2 * atoms
    ring = (SIDE + 2) * layers
    used = (SIDE + 2) * ring
    me_x, me_y = lax.axis_index("gx"), lax.axis_index("gy")
    nx, ny = lax.axis_size("gx"), lax.axis_size("gy")

    def neighbour(d):
        return (lax.rem(me_x + (d // 3 - 1) + nx, nx), lax.rem(me_y + (d % 3 - 1) + ny, ny))

    others = [d for d in range(9) if d != 4]
    barrier = pltpu.get_barrier_semaphore()
    for d in others:
        pl.semaphore_signal(barrier, inc=1, device_id=neighbour(d), device_id_type=pl.DeviceIdType.MESH)

    table[4] = jnp.zeros((ROWS, atoms), F32)
    table[4, 0:3, :] = pos_ref[0, 0]
    table[4, 3:4, :] = spec_ref[0].astype(F32)
    table[4, 4 : 4 + slots, :] = send_ref[0, 0].astype(F32)
    table[4, 7:8, :] = cnt_ref[0].astype(F32)
    table[4, 8:9, 0:bound] = list_ref[0].astype(F32)
    pl.semaphore_wait(barrier, 8)
    copies = []
    for d in others:
        copy = pltpu.make_async_remote_copy(
            src_ref=table.at[4],
            dst_ref=table.at[8 - d],
            send_sem=send_a.at[d],
            recv_sem=recv_a.at[8 - d],
            device_id=neighbour(d),
            device_id_type=pl.DeviceIdType.MESH,
        )
        copy.start()
        copies.append(copy)

    lane = lax.broadcasted_iota(jnp.int32, (1, wide), 1).astype(F32)
    ring_at = lane - atoms
    low_x = ring_at < ring
    long_side = ring_at < 2 * ring
    along = jnp.where(low_x, ring_at, ring_at - ring)
    in_y = ring_at - 2 * ring
    low_y = in_y < column
    across = jnp.where(low_y, in_y, in_y - column)
    half_long = floor_div(along, layers)
    half_short = floor_div(across, layers)
    site_x = jnp.where(long_side, jnp.where(low_x, -1.0, float(SIDE)), half_short)
    site_y = jnp.where(long_side, half_long - 1.0, jnp.where(low_y, -1.0, float(SIDE)))
    site_z = jnp.where(long_side, along - half_long * layers, across - half_short * layers)
    inside = (lane < atoms) | (lane >= used)
    off_x = jnp.where(inside, 0.0, floor_div(site_x, SIDE))
    off_y = jnp.where(inside, 0.0, floor_div(site_y, SIDE))
    ring_atom = (site_x - off_x * SIDE) * column + (site_y - off_y * SIDE) * layers + site_z
    atom_r = jnp.where(lane < atoms, lane, jnp.where(lane >= used, 0.0, ring_atom))
    domain_r = 3.0 * (off_x + 1.0) + (off_y + 1.0)
    hot_r = one_hot_rows(atom_r, atoms)

    wi1, wm1, wo1 = split(wi1_ref[...]), split(wm1_ref[...]), split(wo1_ref[...])
    wi2, wm2, wo2 = split(wi2_ref[...]), split(wm2_ref[...]), split(wo2_ref[...])
    mix = [split(mix_ref[l]) for l in range(3)]
    sqm, mx2, rh = split(sqm_ref[...]), split(mx2_ref[...]), split(rh_ref[...])
    emb = split_three(emb_ref[...])
    ro1_cols = jnp.broadcast_to(ro1_ref[...], (atoms, channels)).T
    ro2_cols = jnp.broadcast_to(ro2_ref[...], (atoms, ro2_ref.shape[1])).T

    for copy in copies:
        copy.wait()

    def tile(x):
        return jnp.concatenate([x] * slots, axis=1)

    def slot(x, k):
        return x[:, k * wide : (k + 1) * wide]

    def own(x):
        return jnp.concatenate([x[:, k * wide : k * wide + atoms] for k in range(slots)], axis=1)

    def own_slot(x, k):
        return x[:, k * atoms : (k + 1) * atoms]

    def spread(x):
        zero = jnp.zeros((x.shape[0], atoms), F32)
        return jnp.concatenate([p for k in range(slots) for p in (own_slot(x, k), zero)], axis=1)

    everything = table[...].reshape(9 * ROWS, atoms)
    parts = split_three(everything)
    rec = by_domain(pick(parts, hot_r), domain_r, ROWS)
    sender = jnp.concatenate([rec[4 + k : 5 + k] for k in range(slots)], axis=1)
    live = jnp.concatenate(
        [jnp.where((rec[7:8] > float(k)) & (lane < used), 1.0, 0.0) for k in range(slots)], axis=1
    )
    is_local = sender < atoms
    ghost = sender - atoms
    block = floor_div(ghost, bound)
    place = ghost - block * bound
    block = jnp.where(block >= 4.0, block + 1.0, block)
    block = jnp.where(is_local, 4.0, block)
    block_x = floor_div(block, 3)
    block_y = block - 3.0 * block_x - 1.0
    block_x = block_x - 1.0
    to_x = tile(off_x) + block_x
    to_y = tile(off_y) + block_y
    domain_s = 3.0 * (to_x + 1.0) + (to_y + 1.0)
    lists = dot(parts[0], one_hot_rows(place, atoms))
    listed = jnp.zeros_like(sender)
    for d in range(9):
        listed = listed + jnp.where(domain_s == float(d), lists[d * ROWS + 8 : d * ROWS + 9], 0.0)
    atom_s = jnp.where(is_local, sender, listed)
    hot_s = one_hot_rows(atom_s, atoms)
    upper = jnp.concatenate([table[d, 0:8, :] for d in range(9)], axis=0)
    snd = by_domain(pick(split_three(upper), hot_s), domain_s, 8)

    side_length = SPACING * SIDE
    dx = (snd[0:1] + block_x * side_length) - tile(rec[0:1])
    dy = (snd[1:2] + block_y * side_length) - tile(rec[1:2])
    dz = snd[2:3] - tile(rec[2:3])
    radius = jnp.sqrt(dx * dx + dy * dy + dz * dz + SOFTEN)
    inverse = 1.0 / radius
    ux, uy, uz = dx * inverse, dy * inverse, dz * inverse
    x = jnp.minimum(radius / CUTOFF, 1.0)
    x2 = x * x
    x5 = x2 * x2 * x
    x6 = x5 * x
    envelope = 1.0 + x6 * (-28.0 + x * (48.0 - 21.0 * x))
    slope = jnp.where(radius < CUTOFF, 1.0 / CUTOFF, 0.0)
    d_envelope = x5 * (-168.0 + x * (336.0 - 168.0 * x)) * slope
    orders = (lax.broadcasted_iota(jnp.int32, (nbasis, 1), 0) + 1).astype(F32) * math.pi
    angle = orders * x
    scale = math.sqrt(2.0 / CUTOFF)
    sines = jnp.sin(angle) * scale
    cosines = jnp.cos(angle) * scale
    basis = sines * (inverse * envelope)
    d_basis = cosines * orders * (slope * inverse * envelope) + sines * (
        inverse * d_envelope - inverse * inverse * envelope
    )
    r3, r5, r15 = math.sqrt(3.0), math.sqrt(5.0), math.sqrt(15.0)
    shapes = [
        None,
        r3 * ux,
        r3 * uy,
        r3 * uz,
        r15 * ux * uy,
        r15 * uy * uz,
        0.5 * r5 * (2.0 * uz * uz - ux * ux - uy * uy),
        r15 * ux * uz,
        0.5 * r15 * (ux * ux - uy * uy),
    ]

    def rows_of(w, l):
        return w[l * channels : (l + 1) * channels]

    species_row = lax.broadcasted_iota(jnp.int32, (species, 1), 0).astype(F32)
    hot_es = jnp.where(species_row == snd[3:4], 1.0, 0.0).astype(BF16)
    hot_er = jnp.where(species_row == rec[3:4], 1.0, 0.0).astype(BF16)
    carrier = pick(emb, hot_es) * (live * (1.0 / slots))
    embedded = pick(emb, hot_er)
    edge_one, one_g1, one_g2 = radial(basis, wi1, wm1, wo1)
    carried = [rows_of(edge_one, l) * carrier for l in range(3)]
    moments = []
    for m in range(9):
        term = carried[DEGREE[m]] if m == 0 else carried[DEGREE[m]] * shapes[m]
        total = slot(term, 0)
        for k in range(1, slots):
            total = total + slot(term, k)
        moments.append(total)
    squares = moments[0] * moments[0]
    for m in range(1, 9):
        squares = squares + moments[m] * moments[m]
    features = [mm(mix[0], split(moments[0])) + mm(sqm, split(squares)) + embedded]
    for l in (1, 2):
        mixed = mm(mix[l], split(jnp.concatenate([moments[m] for m in MEMBERS[l]], axis=1)))
        features += [mixed[:, i * wide : (i + 1) * wide] for i in range(len(MEMBERS[l]))]

    live_two = own(live) * (1.0 / slots)
    edge_two, two_g1, two_g2 = radial(own(basis), wi2, wm2, wo2)
    shapes_two = [None] + [own(s) for s in shapes[1:]]
    at_two, to_x2, to_y2 = own(atom_s), own(to_x), own(to_y)
    ax = floor_div(at_two, column)
    rest = at_two - ax * column
    ay = floor_div(rest, layers)
    az = rest - ay * layers
    sx = ax + to_x2 * SIDE
    sy = ay + to_y2 * SIDE
    outside = jnp.where(
        to_x2 != 0.0,
        jnp.where(to_x2 < 0.0, 0.0, float(ring)) + (sy + 1.0) * layers + az,
        2.0 * ring + jnp.where(to_y2 < 0.0, 0.0, float(column)) + sx * layers + az,
    )
    at_ring = jnp.where((to_x2 == 0.0) & (to_y2 == 0.0), at_two, atoms + outside)
    hot_two = one_hot_rows(at_ring, wide)
    stacked = jnp.concatenate(features, axis=0)
    sent = pick(split(stacked), hot_two)
    projected = []
    for l in range(3):
        total = None
        for m in MEMBERS[l]:
            term = rows_of(sent, m) if m == 0 else rows_of(sent, m) * shapes_two[m]
            total = term if total is None else total + term
        projected.append(total)
    scalar = sum(rows_of(edge_two, l) * projected[l] for l in range(3)) * live_two
    gathered = own_slot(scalar, 0)
    for k in range(1, slots):
        gathered = gathered + own_slot(scalar, k)
    refined = mm(mx2, split(gathered)) + features[0][:, :atoms]
    hidden, hidden_slope = silu_pair(mm(rh, split(refined)))
    energy_two = jnp.sum(ro2_cols * hidden, axis=0, keepdims=True)
    energy_one = jnp.sum(ro1_cols * features[0][:, :atoms], axis=0, keepdims=True)
    owners = jnp.concatenate([own_ref[0, 0, k : k + 1, :].astype(F32) for k in range(slots)], axis=1)
    decay = PAIR * jnp.exp(-own(radius)) * owners * own(live)
    pair = decay * own(envelope)
    energy = energy_one + energy_two
    for k in range(slots):
        energy = energy + own_slot(pair, k)
    energy_ref[0] = energy
    g_radius_pair = decay * (own(d_envelope) - own(envelope))

    g_refined = mm(rh, split(ro2_cols * hidden_slope), TN)
    g_gathered = mm(mx2, split(g_refined), TN)
    t = jnp.concatenate([g_gathered] * slots, axis=1) * live_two
    g_edge_two = jnp.concatenate([t * projected[l] for l in range(3)], axis=0)
    g_proj = [t * rows_of(edge_two, l) for l in range(3)]
    g_sent = jnp.concatenate(
        [g_proj[0]] + [g_proj[DEGREE[m]] * shapes_two[m] for m in range(1, 9)], axis=0
    )
    g_shapes_two = [
        jnp.sum(g_proj[DEGREE[m]] * rows_of(sent, m), axis=0, keepdims=True) for m in range(1, 9)
    ]
    g_basis_two = radial_back(g_edge_two, wi2, wm2, wo2, two_g1, two_g2)
    g_stacked = pick(split(g_sent), hot_two, NT)
    g_features = [rows_of(g_stacked, m) for m in range(9)]
    g_features[0] = g_features[0] + jnp.concatenate(
        [g_refined + ro1_cols, jnp.zeros((channels, wide - atoms), F32)], axis=1
    )

    g_zero = split(g_features[0])
    g_squares = mm(sqm, g_zero, TN) * 2.0
    g_moments = [mm(mix[0], g_zero, TN)]
    for l in (1, 2):
        mixed = mm(mix[l], split(jnp.concatenate([g_features[m] for m in MEMBERS[l]], axis=1)), TN)
        g_moments += [mixed[:, i * wide : (i + 1) * wide] for i in range(len(MEMBERS[l]))]
    g_moments = [g + g_squares * moments[m] for m, g in enumerate(g_moments)]
    g_edge_one = []
    g_shapes = []
    for l in range(3):
        total = None
        for m in MEMBERS[l]:
            tiled = tile(g_moments[m])
            term = tiled if m == 0 else tiled * shapes[m]
            total = term if total is None else total + term
            if m > 0:
                g_shapes.append(jnp.sum(tiled * carried[l], axis=0, keepdims=True))
        g_edge_one.append(total * carrier)
    g_basis = radial_back(jnp.concatenate(g_edge_one, axis=0), wi1, wm1, wo1, one_g1, one_g2)

    g_basis = g_basis + spread(g_basis_two)
    g = [None] + [g_shapes[m] + spread(g_shapes_two[m]) for m in range(8)]
    g_radius = jnp.sum(g_basis * d_basis, axis=0, keepdims=True) + spread(g_radius_pair)
    gux = r3 * g[1] + r15 * (g[4] * uy + g[7] * uz + g[8] * ux) - r5 * ux * g[6]
    guy = r3 * g[2] + r15 * (g[4] * ux + g[5] * uz - g[8] * uy) - r5 * uy * g[6]
    guz = r3 * g[3] + r15 * (g[5] * uy + g[7] * ux) + 2.0 * r5 * uz * g[6]
    radial_part = g_radius - inverse * (gux * ux + guy * uy + guz * uz)
    gd = [inverse * gu + u * radial_part for gu, u in ((gux, ux), (guy, uy), (guz, uz))]
    gd = jnp.concatenate(gd + [jnp.zeros((5, gd[0].shape[1]), F32)], axis=0)
    gr = slot(gd, 0)
    for k in range(1, slots):
        gr = gr + slot(gd, k)
    to_senders = jnp.concatenate([jnp.where(domain_s == float(d), gd, 0.0) for d in range(9)], axis=0)
    to_receivers = jnp.concatenate([jnp.where(domain_r == float(d), gr, 0.0) for d in range(9)], axis=0)
    grads[...] = (
        pick(split_three(to_senders), hot_s, NT) - pick(split_three(to_receivers), hot_r, NT)
    ).reshape(9, 8, atoms)

    copies = []
    for d in others:
        copy = pltpu.make_async_remote_copy(
            src_ref=grads.at[d],
            dst_ref=back.at[8 - d],
            send_sem=send_b.at[d],
            recv_sem=recv_b.at[8 - d],
            device_id=neighbour(d),
            device_id_type=pl.DeviceIdType.MESH,
        )
        copy.start()
        copies.append(copy)
    for copy in copies:
        copy.wait()
    total = grads[4]
    for d in others:
        total = total + back[d]
    force_ref[0, 0] = -total[0:3]


def local(positions, species, senders, counts, owners, send_list, embedding,
          radial_in_one, radial_mid_one, radial_out_one, mixing, square_mix, readout_one,
          radial_in_two, radial_mid_two, radial_out_two, mix_two, read_hidden, read_out):
    atoms = positions.shape[3]
    layers = atoms // (SIDE * SIDE)
    vmem = pl.BlockSpec(memory_space=pltpu.VMEM)
    return pl.pallas_call(
        functools.partial(kernel, layers),
        out_shape=(
            jax.ShapeDtypeStruct(positions.shape, F32),
            jax.ShapeDtypeStruct(counts.shape, F32),
        ),
        in_specs=[vmem] * 19,
        out_specs=(vmem, vmem),
        scratch_shapes=[
            pltpu.VMEM((9, ROWS, atoms), F32),
            pltpu.VMEM((9, 8, atoms), F32),
            pltpu.VMEM((9, 8, atoms), F32),
            pltpu.SemaphoreType.DMA((9,)),
            pltpu.SemaphoreType.DMA((9,)),
            pltpu.SemaphoreType.DMA((9,)),
            pltpu.SemaphoreType.DMA((9,)),
        ],
        compiler_params=pltpu.CompilerParams(
            collective_id=0, has_side_effects=True, vmem_limit_bytes=48 * 1024 * 1024
        ),
    )(
        positions, species, senders, counts, owners, send_list, embedding,
        radial_in_one, radial_mid_one, radial_out_one, mixing, square_mix, readout_one[None],
        radial_in_two, radial_mid_two, radial_out_two, mix_two, read_hidden, read_out[None],
    )


def solution(mesh):
    per_domain = (
        P("gx", "gy", None, None),
        P("gx", "gy", None),
        P("gx", "gy", None, None),
        P("gx", "gy", None),
        P("gx", "gy", None, None),
        P("gx", "gy", None),
    )
    return jax.shard_map(
        local,
        mesh=mesh,
        in_specs=per_domain + (P(),) * 13,
        out_specs=(P("gx", "gy", None, None), P("gx", "gy", None)),
        check_vma=False,
    )
```

time: 203 us -> 33.2 us (0.16)
  waiting for transfers between devices: 80.6 us -> 0 us
  other arithmetic: 32.6 us -> 0 us
  matrix products: 27 us -> 0 us
  local copies, waits for them, and re-layouts: 33.7 us -> 7.17 us
  starting transfers between devices: 25.1 us -> 0 us
  Pallas kernels: 0 us -> 24.9 us
    ppermute x16 -> x0, waiting for transfers between devices: 80.6 us -> none  [the longest x8 46.9 us: from_behind(): return lax.ppermute(value, axis, pairs)]
    dot_general x36 -> x0, matrix products: 27 us -> none  [the longest x24 16.9 us: product(): jnp.dot(left_side, right_side, precision=precise, preferred_element_type=...]
    ppermute x16 -> x0, starting transfers between devices: 25.1 us -> none  [the longest x8 13.4 us: from_behind(): return lax.ppermute(value, axis, pairs)]
    pallas_call x0 -> x1, Pallas kernels: none -> 24.9 us  [local(): pl.pallas_call(functools.partial(kernel, layers), out_shape=(jax.ShapeDty...]
    scatter-add x5 -> x0, other arithmetic: 14.2 us -> none  [the longest x1 5.87 us: layer_two(): jnp.concatenate([features, ghost_features], axis=1)[:, table_index]]
    gather x9 -> x0, local copies, waits for them, and re-layouts: 10.2 us -> none  [the longest x2 5.01 us: layer_two(): jnp.concatenate([features, ghost_features], axis=1)[:, table_index]]
    split x15 -> x0, local copies, waits for them, and re-layouts: 3.68 us -> none  [the longest x6 2.59 us: layer_one(): jnp.concatenate([scalar_feature[None], vectors, tensors], 0)]
    reshape x8 -> x0, local copies, waits for them, and re-layouts: 3.38 us -> none  [the longest x1 1.92 us: layer_two(): jnp.concatenate([features, ghost_features], axis=1)[:, table_index]]
  transfers between devices with their start and end apart: 16 -> 0, of which waited for: 11 -> 0; matrix products, arithmetic and copies ran while one was open for 6% -> 0% of each run, Pallas kernels for 0% -> 0%
where the time goes in v1:
time: 33.2 us; the launch traced here: 32.9 us
  Pallas kernels  24.9 us (75%)
  local copies, waits for them, and re-layouts  7.17 us (22%)
  between operations  0.8 us (2%)
    pallas_call x1, Pallas kernels, local(): pl.pallas_call(functools.partial(kernel, layers), out_shape=(jax.ShapeDty...  24.9 us
    unnamed x35, local copies, waits for them, and re-layouts  6.6 us

profile of v1, /device:TPU:1, one launch (start us, length us, event | category | flops | bytes accessed | tf_op | source)
XLA Modules:
  0.0 32.9 jit_solution(2796673135173867059)
XLA Ops:
  0.6 0.0 copy-start.11
  0.6 0.7 %copy.21.pos_ref = f32[1,1,3,128]{3,2,1,0:T(4,128)S(1)} copy(f32[1,1,3,128]{3,1,2,0:T(1,128)} %param.19) | data formatting | bytes 3072 | tf_op args[0]
  1.4 0.7 %copy.22.send_ref = s32[1,1,3,128]{3,2,1,0:T(4,128)S(1)} copy(s32[1,1,3,128]{3,1,2,0:T(1,128)} %param.21) | data formatting | bytes 3072 | tf_op args[2]
  2.0 0.7 %copy.23.own_ref = s32[1,1,3,128]{3,2,1,0:T(4,128)S(1)} copy(s32[1,1,3,128]{3,1,2,0:T(1,128)} %param.23) | data formatting | bytes 3072 | tf_op args[4]
  2.7 0.8 %copy.25.wi1_ref = f32[64,8]{1,0:T(8,128)S(1)} copy(f32[64,8]{0,1:T(8,128)} %param.26) | data formatting | bytes 4096 | tf_op args[7]
  3.5 0.8 %copy.27.wi2_ref = f32[64,8]{1,0:T(8,128)S(1)} copy(f32[64,8]{0,1:T(8,128)} %param.32) | data formatting | bytes 4096 | tf_op args[13]
  4.3 0.8 %copy.24.emb_ref = f32[128,5]{1,0:T(8,128)S(1)} copy(f32[128,5]{0,1:T(8,128)} %param.25) | data formatting | bytes 5120 | tf_op args[6]
  5.1 0.0 copy-done.11
  5.1 0.0 copy-start.12
  5.1 0.0 copy-start.2
  5.1 0.0 copy-start.4
  5.1 0.0 copy-start.5
  5.1 0.0 copy-start.6
  5.1 0.0 copy-start.7
  5.1 0.0 copy-start.8
  5.1 0.0 copy-start.9
  5.2 0.0 copy-start.10
  5.2 0.1 copy.26.wo1_ref
  5.3 0.7 %copy-done.12 = f32[384,64]{0,1:T(8,128)S(1)} copy-done((f32[384,64]{0,1:T(8,128)S(1)}, f32[384,64]{0,1:T(8,128)}, u32[]{:S(2)}) %copy-start.12) | copy-done | bytes 98328
  6.0 0.0 copy-start
  6.0 0.0 copy-start.1
  6.0 0.0 copy-start.3
  6.0 0.1 copy.28.wo2_ref
  6.1 0.0 copy-done.2
  6.1 0.0 copy-done.4
  6.1 0.0 copy-done.5
  6.1 0.0 copy-done.6
  6.1 0.0 copy-done.7
  6.1 0.0 copy-done.8
  6.1 0.0 copy-done.9
  6.2 0.0 copy-done.10
  6.2 0.7 %copy-done = f32[3,128,128]{2,1,0:T(8,128)S(1)} copy-done((f32[3,128,128]{2,1,0:T(8,128)S(1)}, f32[3,128,128]{2,1,0:T(8,128)}, u32[]{:S(2)}) %copy-start) | copy-done | bytes 196632
  6.9 0.0 copy-done.1
  6.9 0.0 copy-done.3
  6.9 24.9 %shard_map.194 = (f32[1,1,3,128]{3,2,1,0:T(4,128)S(1)}, f32[1,1,128]{2,1,0:T(1,128)S(1)}) custom-call(f32[1,1,3,128]{3,2,1,0:T(4,128)S(1)} %copy.21.pos_ref, s32[1,1,128]{2,1,0:T(1,128)S(1)} %copy-done.6, s32[1,1,3,128]{3,2,1,0:T(4,128)S(1)} %copy.22.send_ref, s32[1,1,128]{2,1,0:T(1,128)S(1)} %copy-done.7, s32[1,1,3,128]{3,2,1,0:T(4,128)S(1)} %copy.23.own_ref, ...), custom_call_target="tpu_custom_call" | custom-call | tf_op jit(solution)/shard_map/pallas_call | solution.py:396
  31.8 0.6 %copy.29 = f32[1,1,3,128]{3,1,2,0:T(1,128)} copy(f32[1,1,3,128]{3,2,1,0:T(4,128)S(1)} %get-tuple-element.2) | data formatting | bytes 3072 | tf_op jit(solution)/shard_map/pallas_call | solution.py:396
  32.4 0.5 %copy.31 = f32[1,1,128]{2,1,0:T(1,128)} copy(f32[1,1,128]{2,1,0:T(1,128)S(1)} %get-tuple-element.7) | data formatting | bytes 1024
Async XLA Ops:
  0.6 4.4 %copy-start.11 = (f32[384,64]{0,1:T(8,128)S(1)}, f32[384,64]{0,1:T(8,128)}, u32[]{:S(2)}) copy-start(f32[384,64]{0,1:T(8,128)} %param.28) | copy-start | bytes 294916
  5.1 0.9 %copy-start.12 = (f32[384,64]{0,1:T(8,128)S(1)}, f32[384,64]{0,1:T(8,128)}, u32[]{:S(2)}) copy-start(f32[384,64]{0,1:T(8,128)} %param.34) | copy-start | bytes 294916
  5.1 1.0 %copy-start.2 = (f32[128,128]{1,0:T(8,128)S(1)}, f32[128,128]{1,0:T(8,128)}, u32[]{:S(2)}) copy-start(f32[128,128]{1,0:T(8,128)} %mx2_ref.1) | copy-start | bytes 196612
  5.1 1.0 %copy-start.4 = (f32[64,64]{1,0:T(8,128)S(1)}, f32[64,64]{1,0:T(8,128)}, u32[]{:S(2)}) copy-start(f32[64,64]{1,0:T(8,128)} %wm2_ref.1) | copy-start | bytes 49156
  5.1 1.0 %copy-start.5 = (f32[16,128]{1,0:T(8,128)S(1)}, f32[16,128]{1,0:T(8,128)}, u32[]{:S(2)}) copy-start(f32[16,128]{1,0:T(8,128)} %rh_ref.1) | copy-start | bytes 24580
  5.1 1.0 %copy-start.6 = (s32[1,1,128]{2,1,0:T(1,128)S(1)}, s32[1,1,128]{2,1,0:T(1,128)}, u32[]{:S(2)}) copy-start(s32[1,1,128]{2,1,0:T(1,128)} %spec_ref.1) | copy-start | bytes 1540
  5.1 1.0 %copy-start.7 = (s32[1,1,128]{2,1,0:T(1,128)S(1)}, s32[1,1,128]{2,1,0:T(1,128)}, u32[]{:S(2)}) copy-start(s32[1,1,128]{2,1,0:T(1,128)} %cnt_ref.1) | copy-start | bytes 1540
  5.1 1.0 %copy-start.8 = (s32[1,1,64]{2,1,0:T(1,128)S(1)}, s32[1,1,64]{2,1,0:T(1,128)}, u32[]{:S(2)}) copy-start(s32[1,1,64]{2,1,0:T(1,128)} %list_ref.1) | copy-start | bytes 772
  5.1 1.0 %copy-start.9 = (f32[128]{0:T(128)S(1)}, f32[128]{0:T(128)}, u32[]{:S(2)}) copy-start(f32[128]{0:T(128)} %param.31) | copy-start | bytes 1540
  5.2 1.0 %copy-start.10 = (f32[16]{0:T(128)S(1)}, f32[16]{0:T(128)}, u32[]{:S(2)}) copy-start(f32[16]{0:T(128)} %param.37) | copy-start | bytes 196
  6.0 0.9 %copy-start = (f32[3,128,128]{2,1,0:T(8,128)S(1)}, f32[3,128,128]{2,1,0:T(8,128)}, u32[]{:S(2)}) copy-start(f32[3,128,128]{2,1,0:T(8,128)} %mix_ref.1) | copy-start | bytes 589828
  6.0 0.9 %copy-start.1 = (f32[128,128]{1,0:T(8,128)S(1)}, f32[128,128]{1,0:T(8,128)}, u32[]{:S(2)}) copy-start(f32[128,128]{1,0:T(8,128)} %sqm_ref.1) | copy-start | bytes 196612
  6.0 0.9 %copy-start.3 = (f32[64,64]{1,0:T(8,128)S(1)}, f32[64,64]{1,0:T(8,128)}, u32[]{:S(2)}) copy-start(f32[64,64]{1,0:T(8,128)} %wm1_ref.1) | copy-start | bytes 49156

commit v2 on v1

--- a/solution.py
+++ b/solution.py
@@ -19,7 +19,6 @@
 F32 = jnp.float32
 BF16 = jnp.bfloat16
 NN = (((1,), (0,)), ((), ()))
-TN = (((0,), (0,)), ((), ()))
 NT = (((1,), (1,)), ((), ()))
 
 
@@ -38,15 +37,43 @@
     return (high,) + split(rest)
 
 
-def mm(a, b, dims=NN):
-    return dot(a[0], b[0], dims) + (dot(a[0], b[1], dims) + dot(a[1], b[0], dims))
-
-
-def pick(parts, one_hot, dims=NN):
-    out = dot(parts[-1], one_hot, dims)
-    for part in parts[-2::-1]:
-        out = out + dot(part, one_hot, dims)
-    return out
+def stack_left(x):
+    high, low = split(x)
+    high, low = high.astype(F32), low.astype(F32)
+    return jnp.concatenate([high, low, high], axis=0).T.astype(BF16)
+
+
+def mm(left, b):
+    high = b.astype(BF16).astype(F32)
+    low = b - high
+    if b.shape[0] % 16:
+        right = jnp.concatenate([high, high, low], axis=0).astype(BF16)
+    else:
+        high, low = high.astype(BF16), low.astype(BF16)
+        right = jnp.concatenate([high, high, low], axis=0)
+    return dot(left, right)
+
+
+def pick(parts, one_hot):
+    return dot(jnp.concatenate(parts, axis=1), jnp.concatenate([one_hot] * len(parts), axis=0))
+
+
+def put(parts, one_hot):
+    return dot(jnp.concatenate(parts, axis=1), jnp.concatenate([one_hot] * len(parts), axis=1), NT)
+
+
+def sin_cos_pi(t):
+    turn = jnp.floor(t + 0.5)
+    r = (t - turn) * math.pi
+    sign = 1.0 - 2.0 * (turn - 2.0 * jnp.floor(turn * 0.5))
+    z = r * r
+    sine = jnp.full_like(z, 1.0 / math.factorial(13))
+    cosine = jnp.full_like(z, -1.0 / math.factorial(14))
+    for n in range(5, -1, -1):
+        sine = sine * z + (-1.0) ** n / math.factorial(2 * n + 1)
+    for n in range(6, -1, -1):
+        cosine = cosine * z + (-1.0) ** n / math.factorial(2 * n)
+    return sign * r * sine, sign * cosine
 
 
 def floor_div(x, by):
@@ -66,36 +93,38 @@
 
 
 def silu_pair(h):
-    gate = jax.nn.sigmoid(h)
+    gate = 0.5 + 0.5 * jnp.tanh(0.5 * h)
     return h * gate, gate * (1.0 + h * (1.0 - gate))
 
 
 def radial(basis, w_in, w_mid, w_out):
-    s1, g1 = silu_pair(mm(w_in, split(basis)))
-    s2, g2 = silu_pair(mm(w_mid, split(s1)))
-    return mm(w_out, split(s2)), g1, g2
+    s1, g1 = silu_pair(mm(w_in, basis))
+    s2, g2 = silu_pair(mm(w_mid, s1))
+    return mm(w_out, s2), g1, g2
 
 
 def radial_back(g_out, w_in, w_mid, w_out, g1, g2):
-    gh2 = mm(w_out, split(g_out), TN) * g2
-    gh1 = mm(w_mid, split(gh2), TN) * g1
-    return mm(w_in, split(gh1), TN)
+    gh2 = mm(w_out, g_out) * g2
+    gh1 = mm(w_mid, gh2) * g1
+    return mm(w_in, gh1)
 
 
 def kernel(
     layers,
-    pos_ref, spec_ref, send_ref, cnt_ref, own_ref, list_ref, emb_ref,
-    wi1_ref, wm1_ref, wo1_ref, mix_ref, sqm_ref, ro1_ref,
-    wi2_ref, wm2_ref, wo2_ref, mx2_ref, rh_ref, ro2_ref,
-    force_ref, energy_ref,
-    table, grads, back, send_a, recv_a, send_b, recv_b,
+    *refs,
 ):
+    inputs, (force_ref, energy_ref), held = refs[:19], refs[19:21], refs[21:40]
+    table, grads, back, load, send_a, recv_a, send_b, recv_b = refs[40:]
+    (
+        pos_ref, spec_ref, send_ref, cnt_ref, list_ref, own_ref, emb_ref,
+        wi1_ref, wm1_ref, wo1_ref, mix_ref, sqm_ref, ro1_ref,
+        wi2_ref, wm2_ref, wo2_ref, mx2_ref, rh_ref, ro2_ref,
+    ) = held
     atoms = pos_ref.shape[3]
     bound = list_ref.shape[2]
-    slots = send_ref.shape[2]
-    channels = emb_ref.shape[0]
-    species = emb_ref.shape[1]
-    nbasis = wi1_ref.shape[1]
+    slots = send_ref.shape[1]
+    species, channels = emb_ref.shape
+    nbasis = wi1_ref.shape[0]
     column = SIDE * layers
     wide = 2 * atoms
     ring = (SIDE + 2) * layers
@@ -111,10 +140,17 @@
     for d in others:
         pl.semaphore_signal(barrier, inc=1, device_id=neighbour(d), device_id_type=pl.DeviceIdType.MESH)
 
+    loads = [pltpu.make_async_copy(inputs[i], held[i], load.at[i]) for i in range(19)]
+    for copy in loads:
+        copy.start()
     table[4] = jnp.zeros((ROWS, atoms), F32)
-    table[4, 0:3, :] = pos_ref[0, 0]
+    for copy in loads[:5]:
+        copy.wait()
+    for k in range(3):
+        table[4, k : k + 1, :] = pos_ref[0, k]
     table[4, 3:4, :] = spec_ref[0].astype(F32)
-    table[4, 4 : 4 + slots, :] = send_ref[0, 0].astype(F32)
+    for k in range(slots):
+        table[4, 4 + k : 5 + k, :] = send_ref[0, k].astype(F32)
     table[4, 7:8, :] = cnt_ref[0].astype(F32)
     table[4, 8:9, 0:bound] = list_ref[0].astype(F32)
     pl.semaphore_wait(barrier, 8)
@@ -152,11 +188,20 @@
     domain_r = 3.0 * (off_x + 1.0) + (off_y + 1.0)
     hot_r = one_hot_rows(atom_r, atoms)
 
-    wi1, wm1, wo1 = split(wi1_ref[...]), split(wm1_ref[...]), split(wo1_ref[...])
-    wi2, wm2, wo2 = split(wi2_ref[...]), split(wm2_ref[...]), split(wo2_ref[...])
-    mix = [split(mix_ref[l]) for l in range(3)]
-    sqm, mx2, rh = split(sqm_ref[...]), split(mx2_ref[...]), split(rh_ref[...])
-    emb = split_three(emb_ref[...])
+    for copy in loads[5:]:
+        copy.wait()
+    wi1, wi1_back = stack_left(wi1_ref[...]), stack_left(wi1_ref[...].T)
+    wi2, wi2_back = stack_left(wi2_ref[...]), stack_left(wi2_ref[...].T)
+    wm1, wm1_back = stack_left(wm1_ref[...].T), stack_left(wm1_ref[...])
+    wm2, wm2_back = stack_left(wm2_ref[...].T), stack_left(wm2_ref[...])
+    wo1, wo1_back = stack_left(wo1_ref[...]), stack_left(wo1_ref[...].T)
+    wo2, wo2_back = stack_left(wo2_ref[...]), stack_left(wo2_ref[...].T)
+    mix = [stack_left(mix_ref[l].T) for l in range(3)]
+    mix_back = [stack_left(mix_ref[l]) for l in range(3)]
+    sqm, sqm_back = stack_left(sqm_ref[...].T), stack_left(sqm_ref[...])
+    mx2, mx2_back = stack_left(mx2_ref[...].T), stack_left(mx2_ref[...])
+    rh, rh_back = stack_left(rh_ref[...].T), stack_left(rh_ref[...])
+    emb = split_three(emb_ref[...].T)
     ro1_cols = jnp.broadcast_to(ro1_ref[...], (atoms, channels)).T
     ro2_cols = jnp.broadcast_to(ro2_ref[...], (atoms, ro2_ref.shape[1])).T
 
@@ -221,13 +266,13 @@
     envelope = 1.0 + x6 * (-28.0 + x * (48.0 - 21.0 * x))
     slope = jnp.where(radius < CUTOFF, 1.0 / CUTOFF, 0.0)
     d_envelope = x5 * (-168.0 + x * (336.0 - 168.0 * x)) * slope
-    orders = (lax.broadcasted_iota(jnp.int32, (nbasis, 1), 0) + 1).astype(F32) * math.pi
-    angle = orders * x
+    orders = (lax.broadcasted_iota(jnp.int32, (nbasis, 1), 0) + 1).astype(F32)
     scale = math.sqrt(2.0 / CUTOFF)
-    sines = jnp.sin(angle) * scale
-    cosines = jnp.cos(angle) * scale
+    sines, cosines = sin_cos_pi(orders * x)
+    sines = sines * scale
+    cosines = cosines * (orders * (scale * math.pi))
     basis = sines * (inverse * envelope)
-    d_basis = cosines * orders * (slope * inverse * envelope) + sines * (
+    d_basis = cosines * (slope * inverse * envelope) + sines * (
         inverse * d_envelope - inverse * inverse * envelope
     )
     r3, r5, r15 = math.sqrt(3.0), math.sqrt(5.0), math.sqrt(15.0)
@@ -263,9 +308,9 @@
     squares = moments[0] * moments[0]
     for m in range(1, 9):
         squares = squares + moments[m] * moments[m]
-    features = [mm(mix[0], split(moments[0])) + mm(sqm, split(squares)) + embedded]
+    features = [mm(mix[0], moments[0]) + mm(sqm, squares) + embedded]
     for l in (1, 2):
-        mixed = mm(mix[l], split(jnp.concatenate([moments[m] for m in MEMBERS[l]], axis=1)))
+        mixed = mm(mix[l], jnp.concatenate([moments[m] for m in MEMBERS[l]], axis=1))
         features += [mixed[:, i * wide : (i + 1) * wide] for i in range(len(MEMBERS[l]))]
 
     live_two = own(live) * (1.0 / slots)
@@ -298,11 +343,11 @@
     gathered = own_slot(scalar, 0)
     for k in range(1, slots):
         gathered = gathered + own_slot(scalar, k)
-    refined = mm(mx2, split(gathered)) + features[0][:, :atoms]
-    hidden, hidden_slope = silu_pair(mm(rh, split(refined)))
+    refined = mm(mx2, gathered) + features[0][:, :atoms]
+    hidden, hidden_slope = silu_pair(mm(rh, refined))
     energy_two = jnp.sum(ro2_cols * hidden, axis=0, keepdims=True)
     energy_one = jnp.sum(ro1_cols * features[0][:, :atoms], axis=0, keepdims=True)
-    owners = jnp.concatenate([own_ref[0, 0, k : k + 1, :].astype(F32) for k in range(slots)], axis=1)
+    owners = jnp.concatenate([own_ref[0, k].astype(F32) for k in range(slots)], axis=1)
     decay = PAIR * jnp.exp(-own(radius)) * owners * own(live)
     pair = decay * own(envelope)
     energy = energy_one + energy_two
@@ -311,8 +356,8 @@
     energy_ref[0] = energy
     g_radius_pair = decay * (own(d_envelope) - own(envelope))
 
-    g_refined = mm(rh, split(ro2_cols * hidden_slope), TN)
-    g_gathered = mm(mx2, split(g_refined), TN)
+    g_refined = mm(rh_back, ro2_cols * hidden_slope)
+    g_gathered = mm(mx2_back, g_refined)
     t = jnp.concatenate([g_gathered] * slots, axis=1) * live_two
     g_edge_two = jnp.concatenate([t * projected[l] for l in range(3)], axis=0)
     g_proj = [t * rows_of(edge_two, l) for l in range(3)]
@@ -322,18 +367,17 @@
     g_shapes_two = [
         jnp.sum(g_proj[DEGREE[m]] * rows_of(sent, m), axis=0, keepdims=True) for m in range(1, 9)
     ]
-    g_basis_two = radial_back(g_edge_two, wi2, wm2, wo2, two_g1, two_g2)
-    g_stacked = pick(split(g_sent), hot_two, NT)
+    g_basis_two = radial_back(g_edge_two, wi2_back, wm2_back, wo2_back, two_g1, two_g2)
+    g_stacked = put(split(g_sent), hot_two)
     g_features = [rows_of(g_stacked, m) for m in range(9)]
     g_features[0] = g_features[0] + jnp.concatenate(
         [g_refined + ro1_cols, jnp.zeros((channels, wide - atoms), F32)], axis=1
     )
 
-    g_zero = split(g_features[0])
-    g_squares = mm(sqm, g_zero, TN) * 2.0
-    g_moments = [mm(mix[0], g_zero, TN)]
+    g_squares = mm(sqm_back, g_features[0]) * 2.0
+    g_moments = [mm(mix_back[0], g_features[0])]
     for l in (1, 2):
-        mixed = mm(mix[l], split(jnp.concatenate([g_features[m] for m in MEMBERS[l]], axis=1)), TN)
+        mixed = mm(mix_back[l], jnp.concatenate([g_features[m] for m in MEMBERS[l]], axis=1))
         g_moments += [mixed[:, i * wide : (i + 1) * wide] for i in range(len(MEMBERS[l]))]
     g_moments = [g + g_squares * moments[m] for m, g in enumerate(g_moments)]
     g_edge_one = []
@@ -347,7 +391,9 @@
             if m > 0:
                 g_shapes.append(jnp.sum(tiled * carried[l], axis=0, keepdims=True))
         g_edge_one.append(total * carrier)
-    g_basis = radial_back(jnp.concatenate(g_edge_one, axis=0), wi1, wm1, wo1, one_g1, one_g2)
+    g_basis = radial_back(
+        jnp.concatenate(g_edge_one, axis=0), wi1_back, wm1_back, wo1_back, one_g1, one_g2
+    )
 
     g_basis = g_basis + spread(g_basis_two)
     g = [None] + [g_shapes[m] + spread(g_shapes_two[m]) for m in range(8)]
@@ -364,7 +410,7 @@
     to_senders = jnp.concatenate([jnp.where(domain_s == float(d), gd, 0.0) for d in range(9)], axis=0)
     to_receivers = jnp.concatenate([jnp.where(domain_r == float(d), gr, 0.0) for d in range(9)], axis=0)
     grads[...] = (
-        pick(split_three(to_senders), hot_s, NT) - pick(split_three(to_receivers), hot_r, NT)
+        put(split(to_senders), hot_s) - put(split(to_receivers), hot_r)
     ).reshape(9, 8, atoms)
 
     copies = []
@@ -384,7 +430,8 @@
     total = grads[4]
     for d in others:
         total = total + back[d]
-    force_ref[0, 0] = -total[0:3]
+    for k in range(3):
+        force_ref[0, k] = -total[k : k + 1]
 
 
 def local(positions, species, senders, counts, owners, send_list, embedding,
@@ -392,32 +439,37 @@
           radial_in_two, radial_mid_two, radial_out_two, mix_two, read_hidden, read_out):
     atoms = positions.shape[3]
     layers = atoms // (SIDE * SIDE)
+    operands = (
+        positions.transpose(0, 2, 1, 3), species, senders.transpose(0, 2, 1, 3), counts, send_list,
+        owners.transpose(0, 2, 1, 3), embedding.T,
+        radial_in_one.T, radial_mid_one, radial_out_one.T, mixing, square_mix, readout_one[None],
+        radial_in_two.T, radial_mid_two, radial_out_two.T, mix_two, read_hidden, read_out[None],
+    )
     vmem = pl.BlockSpec(memory_space=pltpu.VMEM)
-    return pl.pallas_call(
+    forces, energies = pl.pallas_call(
         functools.partial(kernel, layers),
         out_shape=(
-            jax.ShapeDtypeStruct(positions.shape, F32),
+            jax.ShapeDtypeStruct(operands[0].shape, F32),
             jax.ShapeDtypeStruct(counts.shape, F32),
         ),
-        in_specs=[vmem] * 19,
+        in_specs=[pl.BlockSpec(memory_space=pltpu.HBM)] * len(operands),
         out_specs=(vmem, vmem),
-        scratch_shapes=[
+        scratch_shapes=[pltpu.VMEM(x.shape, x.dtype) for x in operands]
+        + [
             pltpu.VMEM((9, ROWS, atoms), F32),
             pltpu.VMEM((9, 8, atoms), F32),
             pltpu.VMEM((9, 8, atoms), F32),
+            pltpu.SemaphoreType.DMA((len(operands),)),
             pltpu.SemaphoreType.DMA((9,)),
             pltpu.SemaphoreType.DMA((9,)),
             pltpu.SemaphoreType.DMA((9,)),
             pltpu.SemaphoreType.DMA((9,)),
         ],
         compiler_params=pltpu.CompilerParams(
-            collective_id=0, has_side_effects=True, vmem_limit_bytes=48 * 1024 * 1024
+            collective_id=0, has_side_effects=True, vmem_limit_bytes=64 * 1024 * 1024
         ),
-    )(
-        positions, species, senders, counts, owners, send_list, embedding,
-        radial_in_one, radial_mid_one, radial_out_one, mixing, square_mix, readout_one[None],
-        radial_in_two, radial_mid_two, radial_out_two, mix_two, read_hidden, read_out[None],
-    )
+    )(*operands)
+    return forces.transpose(0, 2, 1, 3), energies
 
 
 def solution(mesh):

time: 33.2 us -> 26 us (0.78)
  local copies, waits for them, and re-layouts: 7.17 us -> 1.8 us
  Pallas kernels: 24.9 us -> 23.4 us
    unnamed x35 -> x6, local copies, waits for them, and re-layouts: 6.6 us -> 1.8 us
    pallas_call x1, Pallas kernels: 24.9 us -> 23.4 us  [local(): pl.pallas_call(functools.partial(kernel, layers), out_shape=(jax.ShapeDty...]
    pallas_call x1 -> x0, local copies, waits for them, and re-layouts: 0.56 us -> none  [local(): pl.pallas_call(functools.partial(kernel, layers), out_shape=(jax.ShapeDty...]
where the time goes in v2:
time: 26 us; the launch traced here: 25.9 us
  Pallas kernels  23.4 us (90%)
  local copies, waits for them, and re-layouts  1.8 us (7%)
  between operations  0.66 us (3%)
    pallas_call x1, Pallas kernels, local(): pl.pallas_call(functools.partial(kernel, layers), out_shape=(jax.ShapeDty...  23.4 us
    unnamed x6, local copies, waits for them, and re-layouts  1.8 us

profile of v2, /device:TPU:1, one launch (start us, length us, event | category | flops | bytes accessed | tf_op | source)
XLA Modules:
  0.0 25.9 jit_solution(114792637629036262)
XLA Ops:
  0.6 23.4 %shard_map.194 = (f32[1,3,1,128]{3,2,1,0:T(1,128)}, f32[1,1,128]{2,1,0:T(1,128)}) custom-call(f32[1,3,1,128]{3,2,1,0:T(1,128)} %bitcast.18, s32[1,1,128]{2,1,0:T(1,128)} %refs_1_.1, s32[1,3,1,128]{3,2,1,0:T(1,128)} %bitcast.19, s32[1,1,128]{2,1,0:T(1,128)} %refs_3_.1, s32[1,1,64]{2,1,0:T(1,128)} %refs_4_.1, s32[1,3,1,128]{3,2,1,0:T(1,128)} %bitcast.20, ...), custom_call_target="tpu_custom_call" | custom-call | tf_op jit(solution)/shard_map/pallas_call | solution.py:449
  24.0 0.0 copy-start
  24.1 0.7 %copy-done = f32[1,3,1,128]{3,2,1,0:T(1,128)S(1)} copy-done((f32[1,3,1,128]{3,2,1,0:T(1,128)S(1)}, f32[1,3,1,128]{3,2,1,0:T(1,128)}, u32[]{:S(2)}) %copy-start) | copy-done | bytes 1560
  24.7 0.0 copy-start.1
  24.7 0.6 %copy.24 = f32[1,1,3,128]{3,1,2,0:T(1,128)} copy(f32[1,1,3,128]{3,1,2,0:T(1,128)S(1)} %bitcast.21) | data formatting | bytes 3072
  25.3 0.1 copy-done.1
  25.3 0.5 %copy.25 = f32[1,1,128]{2,1,0:T(1,128)} copy(f32[1,1,128]{2,1,0:T(1,128)S(1)} %copy-done.1) | data formatting | bytes 1024
Async XLA Ops:
  24.0 0.7 %copy-start = (f32[1,3,1,128]{3,2,1,0:T(1,128)S(1)}, f32[1,3,1,128]{3,2,1,0:T(1,128)}, u32[]{:S(2)}) copy-start(f32[1,3,1,128]{3,2,1,0:T(1,128)} %get-tuple-element.4) | copy-start | bytes 4612
  24.7 0.6 %copy-start.1 = (f32[1,1,128]{2,1,0:T(1,128)S(1)}, f32[1,1,128]{2,1,0:T(1,128)}, u32[]{:S(2)}) copy-start(f32[1,1,128]{2,1,0:T(1,128)} %get-tuple-element.11) | copy-start | bytes 1540

commit v3 on v2

--- a/solution.py
+++ b/solution.py
@@ -113,8 +113,11 @@
     layers,
     *refs,
 ):
-    inputs, (force_ref, energy_ref), held = refs[:19], refs[19:21], refs[21:40]
-    table, grads, back, load, send_a, recv_a, send_b, recv_b = refs[40:]
+    inputs, out_ref, held = refs[:19], refs[19], refs[20:39]
+    table, grads, back, load, send_a, recv_a, send_b, recv_b = refs[39:47]
+    basis_s, shape_s, edge_s, gate_s, carrier_s, carried_s, moment_s, g_moment_s, g_basis_s, g_shape_s = (
+        refs[47:]
+    )
     (
         pos_ref, spec_ref, send_ref, cnt_ref, list_ref, own_ref, emb_ref,
         wi1_ref, wm1_ref, wo1_ref, mix_ref, sqm_ref, ro1_ref,
@@ -291,20 +294,36 @@
     def rows_of(w, l):
         return w[l * channels : (l + 1) * channels]
 
+    shapes_all = jnp.concatenate(shapes[1:], axis=0)
+    live_one = live * (1.0 / slots)
+    for k in range(slots):
+        basis_s[k] = slot(basis, k)
+        shape_s[k] = slot(shapes_all, k)
+        edge_s[k, 0:1, :] = slot(snd[3:4], k)
+        edge_s[k, 1:2, :] = slot(live_one, k)
     species_row = lax.broadcasted_iota(jnp.int32, (species, 1), 0).astype(F32)
-    hot_es = jnp.where(species_row == snd[3:4], 1.0, 0.0).astype(BF16)
     hot_er = jnp.where(species_row == rec[3:4], 1.0, 0.0).astype(BF16)
-    carrier = pick(emb, hot_es) * (live * (1.0 / slots))
     embedded = pick(emb, hot_er)
-    edge_one, one_g1, one_g2 = radial(basis, wi1, wm1, wo1)
-    carried = [rows_of(edge_one, l) * carrier for l in range(3)]
-    moments = []
-    for m in range(9):
-        term = carried[DEGREE[m]] if m == 0 else carried[DEGREE[m]] * shapes[m]
-        total = slot(term, 0)
-        for k in range(1, slots):
-            total = total + slot(term, k)
-        moments.append(total)
+    moment_s[...] = jnp.zeros(moment_s.shape, F32)
+
+    def forward(k, carry):
+        hot_es = jnp.where(species_row == edge_s[k, 0:1, :], 1.0, 0.0).astype(BF16)
+        carrier = pick(emb, hot_es) * edge_s[k, 1:2, :]
+        carrier_s[k] = carrier
+        edge, g1, g2 = radial(basis_s[k], wi1, wm1, wo1)
+        gate_s[k, 0] = g1
+        gate_s[k, 1] = g2
+        shape = shape_s[k]
+        for l in range(3):
+            carried = rows_of(edge, l) * carrier
+            carried_s[k, l] = carried
+            for m in MEMBERS[l]:
+                term = carried if m == 0 else carried * shape[m - 1 : m]
+                moment_s[m] = moment_s[m] + term
+        return carry
+
+    lax.fori_loop(0, slots, forward, 0)
+    moments = [moment_s[m] for m in range(9)]
     squares = moments[0] * moments[0]
     for m in range(1, 9):
         squares = squares + moments[m] * moments[m]
@@ -353,7 +372,7 @@
     energy = energy_one + energy_two
     for k in range(slots):
         energy = energy + own_slot(pair, k)
-    energy_ref[0] = energy
+    out_ref[0, 3] = energy
     g_radius_pair = decay * (own(d_envelope) - own(envelope))
 
     g_refined = mm(rh_back, ro2_cols * hidden_slope)
@@ -379,21 +398,34 @@
     for l in (1, 2):
         mixed = mm(mix_back[l], jnp.concatenate([g_features[m] for m in MEMBERS[l]], axis=1))
         g_moments += [mixed[:, i * wide : (i + 1) * wide] for i in range(len(MEMBERS[l]))]
-    g_moments = [g + g_squares * moments[m] for m, g in enumerate(g_moments)]
-    g_edge_one = []
-    g_shapes = []
-    for l in range(3):
-        total = None
-        for m in MEMBERS[l]:
-            tiled = tile(g_moments[m])
-            term = tiled if m == 0 else tiled * shapes[m]
-            total = term if total is None else total + term
-            if m > 0:
-                g_shapes.append(jnp.sum(tiled * carried[l], axis=0, keepdims=True))
-        g_edge_one.append(total * carrier)
-    g_basis = radial_back(
-        jnp.concatenate(g_edge_one, axis=0), wi1_back, wm1_back, wo1_back, one_g1, one_g2
-    )
+    for m in range(9):
+        g_moment_s[m] = g_moments[m] + g_squares * moment_s[m]
+
+    def backward(k, carry):
+        carrier = carrier_s[k]
+        shape = shape_s[k]
+        g_edge = []
+        g_shape = []
+        for l in range(3):
+            carried = carried_s[k, l]
+            total = None
+            for m in MEMBERS[l]:
+                g_m = g_moment_s[m]
+                term = g_m if m == 0 else g_m * shape[m - 1 : m]
+                total = term if total is None else total + term
+                if m > 0:
+                    g_shape.append(jnp.sum(g_m * carried, axis=0, keepdims=True))
+            g_edge.append(total * carrier)
+        g_shape_s[k] = jnp.concatenate(g_shape, axis=0)
+        g_basis_s[k] = radial_back(
+            jnp.concatenate(g_edge, axis=0), wi1_back, wm1_back, wo1_back, gate_s[k, 0], gate_s[k, 1]
+        )
+        return carry
+
+    lax.fori_loop(0, slots, backward, 0)
+    g_basis = jnp.concatenate([g_basis_s[k] for k in range(slots)], axis=1)
+    g_shapes_all = jnp.concatenate([g_shape_s[k] for k in range(slots)], axis=1)
+    g_shapes = [g_shapes_all[m : m + 1] for m in range(8)]
 
     g_basis = g_basis + spread(g_basis_two)
     g = [None] + [g_shapes[m] + spread(g_shapes_two[m]) for m in range(8)]
@@ -431,7 +463,18 @@
     for d in others:
         total = total + back[d]
     for k in range(3):
-        force_ref[0, k] = -total[k : k + 1]
+        out_ref[0, k] = -total[k : k + 1]
+
+
+def part(both_ref, force_ref, energy_ref, sems):
+    copies = [
+        pltpu.make_async_copy(both_ref.at[:, 0:3], force_ref, sems.at[0]),
+        pltpu.make_async_copy(both_ref.at[:, 3], energy_ref, sems.at[1]),
+    ]
+    for copy in copies:
+        copy.start()
+    for copy in copies:
+        copy.wait()
 
 
 def local(positions, species, senders, counts, owners, send_list, embedding,
@@ -439,6 +482,9 @@
           radial_in_two, radial_mid_two, radial_out_two, mix_two, read_hidden, read_out):
     atoms = positions.shape[3]
     layers = atoms // (SIDE * SIDE)
+    slots, wide = senders.shape[2], 2 * atoms
+    channels = embedding.shape[0]
+    hidden, nbasis = radial_in_one.shape
     operands = (
         positions.transpose(0, 2, 1, 3), species, senders.transpose(0, 2, 1, 3), counts, send_list,
         owners.transpose(0, 2, 1, 3), embedding.T,
@@ -446,14 +492,11 @@
         radial_in_two.T, radial_mid_two, radial_out_two.T, mix_two, read_hidden, read_out[None],
     )
     vmem = pl.BlockSpec(memory_space=pltpu.VMEM)
-    forces, energies = pl.pallas_call(
+    both = pl.pallas_call(
         functools.partial(kernel, layers),
-        out_shape=(
-            jax.ShapeDtypeStruct(operands[0].shape, F32),
-            jax.ShapeDtypeStruct(counts.shape, F32),
-        ),
+        out_shape=jax.ShapeDtypeStruct((1, 4, 1, atoms), F32),
         in_specs=[pl.BlockSpec(memory_space=pltpu.HBM)] * len(operands),
-        out_specs=(vmem, vmem),
+        out_specs=vmem,
         scratch_shapes=[pltpu.VMEM(x.shape, x.dtype) for x in operands]
         + [
             pltpu.VMEM((9, ROWS, atoms), F32),
@@ -464,11 +507,33 @@
             pltpu.SemaphoreType.DMA((9,)),
             pltpu.SemaphoreType.DMA((9,)),
             pltpu.SemaphoreType.DMA((9,)),
+            pltpu.VMEM((slots, nbasis, wide), F32),
+            pltpu.VMEM((slots, 8, wide), F32),
+            pltpu.VMEM((slots, 8, wide), F32),
+            pltpu.VMEM((slots, 2, hidden, wide), F32),
+            pltpu.VMEM((slots, channels, wide), F32),
+            pltpu.VMEM((slots, 3, channels, wide), F32),
+            pltpu.VMEM((9, channels, wide), F32),
+            pltpu.VMEM((9, channels, wide), F32),
+            pltpu.VMEM((slots, nbasis, wide), F32),
+            pltpu.VMEM((slots, 8, wide), F32),
         ],
         compiler_params=pltpu.CompilerParams(
             collective_id=0, has_side_effects=True, vmem_limit_bytes=64 * 1024 * 1024
         ),
     )(*operands)
+    hbm = pl.BlockSpec(memory_space=pltpu.HBM)
+    forces, energies = pl.pallas_call(
+        part,
+        out_shape=(
+            jax.ShapeDtypeStruct(operands[0].shape, F32),
+            jax.ShapeDtypeStruct(counts.shape, F32),
+        ),
+        in_specs=[hbm],
+        out_specs=(hbm, hbm),
+        scratch_shapes=[pltpu.SemaphoreType.DMA((2,))],
+        compiler_params=pltpu.CompilerParams(vmem_limit_bytes=64 * 1024 * 1024),
+    )(both)
     return forces.transpose(0, 2, 1, 3), energies
 
 

time: 26 us -> 27.6 us (1.062)
  Pallas kernels: 23.4 us -> 26.8 us
  local copies, waits for them, and re-layouts: 1.8 us -> 0 us
    pallas_call x1 -> x2, Pallas kernels: 23.4 us -> 26.8 us  [the longest x1 25.6 us: local(): pl.pallas_call(functools.partial(kernel, layers), out_shape=jax.ShapeDtyp...]
    unnamed x6 -> x0, local copies, waits for them, and re-layouts: 1.8 us -> none
where the time goes in v3:
time: 27.6 us; the launch traced here: 27.4 us
  Pallas kernels  26.8 us (97%)
  between operations  0.65 us (2%)
    pallas_call x1, Pallas kernels, local(): pl.pallas_call(functools.partial(kernel, layers), out_shape=jax.ShapeDtyp...  25.6 us
    pallas_call x1, Pallas kernels, local(): pl.pallas_call(part, out_shape=(jax.ShapeDtypeStruct(operands[0].shape, F...  1.18 us

profile of v3, /device:TPU:1, one launch (start us, length us, event | category | flops | bytes accessed | tf_op | source)
XLA Modules:
  0.0 27.4 jit_solution(18248228012661979420)
XLA Ops:
  0.6 25.6 %shard_map.194.both_ref = f32[1,4,1,128]{3,2,1,0:T(1,128)} custom-call(f32[1,3,1,128]{3,2,1,0:T(1,128)} %bitcast.18, s32[1,1,128]{2,1,0:T(1,128)} %refs_1_.1, s32[1,3,1,128]{3,2,1,0:T(1,128)} %bitcast.19, s32[1,1,128]{2,1,0:T(1,128)} %refs_3_.1, s32[1,1,64]{2,1,0:T(1,128)} %refs_4_.1, s32[1,3,1,128]{3,2,1,0:T(1,128)} %bitcast.20, f32[5,128]{1,0:T(8,128)} %bitcast.15, ...), custom_call_target="tpu_custom_call" | custom-call | tf_op jit(solution)/shard_map/pallas_call | solution.py:495
  26.2 1.2 %shard_map.195 = (f32[1,3,1,128]{3,2,1,0:T(1,128)}, f32[1,1,128]{2,1,0:T(1,128)}) custom-call(f32[1,4,1,128]{3,2,1,0:T(1,128)} %shard_map.194.both_ref), custom_call_target="tpu_custom_call" | custom-call | tf_op jit(solution)/shard_map/pallas_call | solution.py:526

commit v4 on v2

--- a/solution.py
+++ b/solution.py
@@ -43,6 +43,11 @@
     return jnp.concatenate([high, low, high], axis=0).T.astype(BF16)
 
 
+def left(x):
+    high, low = split(x)
+    return jnp.concatenate([high, low, high], axis=1)
+
+
 def mm(left, b):
     high = b.astype(BF16).astype(F32)
     low = b - high
@@ -113,8 +118,8 @@
     layers,
     *refs,
 ):
-    inputs, (force_ref, energy_ref), held = refs[:19], refs[19:21], refs[21:40]
-    table, grads, back, load, send_a, recv_a, send_b, recv_b = refs[40:]
+    inputs, back, held = refs[:19], refs[19], refs[20:39]
+    table, grads, load, send_a, recv_a, send_b, recv_b = refs[39:]
     (
         pos_ref, spec_ref, send_ref, cnt_ref, list_ref, own_ref, emb_ref,
         wi1_ref, wm1_ref, wo1_ref, mix_ref, sqm_ref, ro1_ref,
@@ -194,13 +199,14 @@
     wi2, wi2_back = stack_left(wi2_ref[...]), stack_left(wi2_ref[...].T)
     wm1, wm1_back = stack_left(wm1_ref[...].T), stack_left(wm1_ref[...])
     wm2, wm2_back = stack_left(wm2_ref[...].T), stack_left(wm2_ref[...])
-    wo1, wo1_back = stack_left(wo1_ref[...]), stack_left(wo1_ref[...].T)
-    wo2, wo2_back = stack_left(wo2_ref[...]), stack_left(wo2_ref[...].T)
-    mix = [stack_left(mix_ref[l].T) for l in range(3)]
-    mix_back = [stack_left(mix_ref[l]) for l in range(3)]
-    sqm, sqm_back = stack_left(sqm_ref[...].T), stack_left(sqm_ref[...])
-    mx2, mx2_back = stack_left(mx2_ref[...].T), stack_left(mx2_ref[...])
-    rh, rh_back = stack_left(rh_ref[...].T), stack_left(rh_ref[...])
+    wo1, wo1_back = stack_left(wo1_ref[...]), left(wo1_ref[...])
+    wo2, wo2_back = stack_left(wo2_ref[...]), left(wo2_ref[...])
+    mix = [left(mix_ref[l]) for l in range(3)]
+    mix_back = [left(mix_ref[l].T) for l in range(3)]
+    sqm, sqm_back = left(sqm_ref[...]), left(sqm_ref[...].T)
+    rh, rh_back = left(rh_ref[...]), stack_left(rh_ref[...])
+    joined = mm(rh, mx2_ref[...])
+    both, both_back = left(joined), stack_left(joined)
     emb = split_three(emb_ref[...].T)
     ro1_cols = jnp.broadcast_to(ro1_ref[...], (atoms, channels)).T
     ro2_cols = jnp.broadcast_to(ro2_ref[...], (atoms, ro2_ref.shape[1])).T
@@ -343,8 +349,7 @@
     gathered = own_slot(scalar, 0)
     for k in range(1, slots):
         gathered = gathered + own_slot(scalar, k)
-    refined = mm(mx2, gathered) + features[0][:, :atoms]
-    hidden, hidden_slope = silu_pair(mm(rh, refined))
+    hidden, hidden_slope = silu_pair(mm(both, gathered) + mm(rh, features[0][:, :atoms]))
     energy_two = jnp.sum(ro2_cols * hidden, axis=0, keepdims=True)
     energy_one = jnp.sum(ro1_cols * features[0][:, :atoms], axis=0, keepdims=True)
     owners = jnp.concatenate([own_ref[0, k].astype(F32) for k in range(slots)], axis=1)
@@ -353,11 +358,11 @@
     energy = energy_one + energy_two
     for k in range(slots):
         energy = energy + own_slot(pair, k)
-    energy_ref[0] = energy
     g_radius_pair = decay * (own(d_envelope) - own(envelope))
 
-    g_refined = mm(rh_back, ro2_cols * hidden_slope)
-    g_gathered = mm(mx2_back, g_refined)
+    g_hidden = ro2_cols * hidden_slope
+    g_refined = mm(rh_back, g_hidden)
+    g_gathered = mm(both_back, g_hidden)
     t = jnp.concatenate([g_gathered] * slots, axis=1) * live_two
     g_edge_two = jnp.concatenate([t * projected[l] for l in range(3)], axis=0)
     g_proj = [t * rows_of(edge_two, l) for l in range(3)]
@@ -412,7 +417,6 @@
     grads[...] = (
         put(split(to_senders), hot_s) - put(split(to_receivers), hot_r)
     ).reshape(9, 8, atoms)
-
     copies = []
     for d in others:
         copy = pltpu.make_async_remote_copy(
@@ -425,13 +429,20 @@
         )
         copy.start()
         copies.append(copy)
-    for copy in copies:
+    grads[4, 3:4, :] = energy
+    copy = pltpu.make_async_copy(grads.at[4], back.at[4], send_b.at[4])
+    copy.start()
+    for copy in copies + [copy]:
         copy.wait()
-    total = grads[4]
-    for d in others:
-        total = total + back[d]
+
+
+def settle(back_ref, force_ref, energy_ref):
+    total = back_ref[0]
+    for d in range(1, 9):
+        total = total + back_ref[d]
     for k in range(3):
         force_ref[0, k] = -total[k : k + 1]
+    energy_ref[0] = back_ref[4, 3:4, :]
 
 
 def local(positions, species, senders, counts, owners, send_list, embedding,
@@ -446,18 +457,15 @@
         radial_in_two.T, radial_mid_two, radial_out_two.T, mix_two, read_hidden, read_out[None],
     )
     vmem = pl.BlockSpec(memory_space=pltpu.VMEM)
-    forces, energies = pl.pallas_call(
+    hbm = pl.BlockSpec(memory_space=pltpu.HBM)
+    back = pl.pallas_call(
         functools.partial(kernel, layers),
-        out_shape=(
-            jax.ShapeDtypeStruct(operands[0].shape, F32),
-            jax.ShapeDtypeStruct(counts.shape, F32),
-        ),
-        in_specs=[pl.BlockSpec(memory_space=pltpu.HBM)] * len(operands),
-        out_specs=(vmem, vmem),
+        out_shape=jax.ShapeDtypeStruct((9, 8, atoms), F32),
+        in_specs=[hbm] * len(operands),
+        out_specs=hbm,
         scratch_shapes=[pltpu.VMEM(x.shape, x.dtype) for x in operands]
         + [
             pltpu.VMEM((9, ROWS, atoms), F32),
-            pltpu.VMEM((9, 8, atoms), F32),
             pltpu.VMEM((9, 8, atoms), F32),
             pltpu.SemaphoreType.DMA((len(operands),)),
             pltpu.SemaphoreType.DMA((9,)),
@@ -469,6 +477,16 @@
             collective_id=0, has_side_effects=True, vmem_limit_bytes=64 * 1024 * 1024
         ),
     )(*operands)
+    forces, energies = pl.pallas_call(
+        settle,
+        out_shape=(
+            jax.ShapeDtypeStruct(operands[0].shape, F32),
+            jax.ShapeDtypeStruct(counts.shape, F32),
+        ),
+        in_specs=[vmem],
+        out_specs=(vmem, vmem),
+        compiler_params=pltpu.CompilerParams(vmem_limit_bytes=64 * 1024 * 1024),
+    )(back)
     return forces.transpose(0, 2, 1, 3), energies
 
 

time: 26 us -> 24.7 us (0.950)
  local copies, waits for them, and re-layouts: 1.8 us -> 0 us
  Pallas kernels: 23.4 us -> 23.9 us
    unnamed x6 -> x0, local copies, waits for them, and re-layouts: 1.8 us -> none
    pallas_call x1 -> x2, Pallas kernels: 23.4 us -> 23.9 us  [the longest x1 22.5 us: local(): pl.pallas_call(functools.partial(kernel, layers), out_shape=jax.ShapeDtyp...]
where the time goes in v4:
time: 24.7 us; the launch traced here: 24.5 us
  Pallas kernels  23.9 us (97%)
  between operations  0.65 us (3%)
    pallas_call x1, Pallas kernels, local(): pl.pallas_call(functools.partial(kernel, layers), out_shape=jax.ShapeDtyp...  22.5 us
    pallas_call x1, Pallas kernels, local(): pl.pallas_call(settle, out_shape=(jax.ShapeDtypeStruct(operands[0].shape,...  1.34 us

profile of v4, /device:TPU:1, one launch (start us, length us, event | category | flops | bytes accessed | tf_op | source)
XLA Modules:
  0.0 24.5 jit_solution(15397399965658352097)
XLA Ops:
  0.6 22.5 %shard_map.194.back_ref = f32[9,8,128]{2,1,0:T(8,128)} custom-call(f32[1,3,1,128]{3,2,1,0:T(1,128)} %bitcast.18, s32[1,1,128]{2,1,0:T(1,128)} %refs_1_.1, s32[1,3,1,128]{3,2,1,0:T(1,128)} %bitcast.19, s32[1,1,128]{2,1,0:T(1,128)} %refs_3_.1, s32[1,1,64]{2,1,0:T(1,128)} %refs_4_.1, s32[1,3,1,128]{3,2,1,0:T(1,128)} %bitcast.20, f32[5,128]{1,0:T(8,128)} %bitcast.15, ...), custom_call_target="tpu_custom_call" | custom-call | tf_op jit(solution)/shard_map/pallas_call | solution.py:461
  23.2 1.3 %shard_map.195 = (f32[1,3,1,128]{3,2,1,0:T(1,128)}, f32[1,1,128]{2,1,0:T(1,128)}) custom-call(f32[9,8,128]{2,1,0:T(8,128)} %shard_map.194.back_ref), custom_call_target="tpu_custom_call" | custom-call | tf_op jit(solution)/shard_map/pallas_call | solution.py:480

commit v5 on v4

--- a/solution.py
+++ b/solution.py
@@ -45,7 +45,14 @@
 
 def left(x):
     high, low = split(x)
-    return jnp.concatenate([high, low, high], axis=1)
+    lower = jnp.concatenate([low, jnp.zeros_like(low)], axis=1)
+    return jnp.concatenate([jnp.concatenate([high, high], axis=1), lower], axis=0)
+
+
+def mm_rows(left, b):
+    out = dot(left, jnp.concatenate(split(b), axis=0))
+    half = left.shape[0] // 2
+    return out[:half] + out[half:]
 
 
 def mm(left, b):
@@ -109,7 +116,7 @@
 
 
 def radial_back(g_out, w_in, w_mid, w_out, g1, g2):
-    gh2 = mm(w_out, g_out) * g2
+    gh2 = mm_rows(w_out, g_out) * g2
     gh1 = mm(w_mid, gh2) * g1
     return mm(w_in, gh1)
 
@@ -205,7 +212,7 @@
     mix_back = [left(mix_ref[l].T) for l in range(3)]
     sqm, sqm_back = left(sqm_ref[...]), left(sqm_ref[...].T)
     rh, rh_back = left(rh_ref[...]), stack_left(rh_ref[...])
-    joined = mm(rh, mx2_ref[...])
+    joined = mm_rows(rh, mx2_ref[...])
     both, both_back = left(joined), stack_left(joined)
     emb = split_three(emb_ref[...].T)
     ro1_cols = jnp.broadcast_to(ro1_ref[...], (atoms, channels)).T
@@ -314,9 +321,9 @@
     squares = moments[0] * moments[0]
     for m in range(1, 9):
         squares = squares + moments[m] * moments[m]
-    features = [mm(mix[0], moments[0]) + mm(sqm, squares) + embedded]
+    features = [mm_rows(mix[0], moments[0]) + mm_rows(sqm, squares) + embedded]
     for l in (1, 2):
-        mixed = mm(mix[l], jnp.concatenate([moments[m] for m in MEMBERS[l]], axis=1))
+        mixed = mm_rows(mix[l], jnp.concatenate([moments[m] for m in MEMBERS[l]], axis=1))
         features += [mixed[:, i * wide : (i + 1) * wide] for i in range(len(MEMBERS[l]))]
 
     live_two = own(live) * (1.0 / slots)
@@ -349,7 +356,7 @@
     gathered = own_slot(scalar, 0)
     for k in range(1, slots):
         gathered = gathered + own_slot(scalar, k)
-    hidden, hidden_slope = silu_pair(mm(both, gathered) + mm(rh, features[0][:, :atoms]))
+    hidden, hidden_slope = silu_pair(mm_rows(both, gathered) + mm_rows(rh, features[0][:, :atoms]))
     energy_two = jnp.sum(ro2_cols * hidden, axis=0, keepdims=True)
     energy_one = jnp.sum(ro1_cols * features[0][:, :atoms], axis=0, keepdims=True)
     owners = jnp.concatenate([own_ref[0, k].astype(F32) for k in range(slots)], axis=1)
@@ -379,10 +386,10 @@
         [g_refined + ro1_cols, jnp.zeros((channels, wide - atoms), F32)], axis=1
     )
 
-    g_squares = mm(sqm_back, g_features[0]) * 2.0
-    g_moments = [mm(mix_back[0], g_features[0])]
+    g_squares = mm_rows(sqm_back, g_features[0]) * 2.0
+    g_moments = [mm_rows(mix_back[0], g_features[0])]
     for l in (1, 2):
-        mixed = mm(mix_back[l], jnp.concatenate([g_features[m] for m in MEMBERS[l]], axis=1))
+        mixed = mm_rows(mix_back[l], jnp.concatenate([g_features[m] for m in MEMBERS[l]], axis=1))
         g_moments += [mixed[:, i * wide : (i + 1) * wide] for i in range(len(MEMBERS[l]))]
     g_moments = [g + g_squares * moments[m] for m, g in enumerate(g_moments)]
     g_edge_one = []
@@ -412,11 +419,13 @@
     gr = slot(gd, 0)
     for k in range(1, slots):
         gr = gr + slot(gd, k)
-    to_senders = jnp.concatenate([jnp.where(domain_s == float(d), gd, 0.0) for d in range(9)], axis=0)
-    to_receivers = jnp.concatenate([jnp.where(domain_r == float(d), gr, 0.0) for d in range(9)], axis=0)
-    grads[...] = (
-        put(split(to_senders), hot_s) - put(split(to_receivers), hot_r)
-    ).reshape(9, 8, atoms)
+    to_senders = jnp.concatenate([jnp.where(domain_s == float(d), gd, 0.0) for d in range(10)], axis=0)
+    to_receivers = jnp.concatenate([jnp.where(domain_r == float(d), gr, 0.0) for d in range(10)], axis=0)
+    to_all = jnp.concatenate(
+        split(jnp.concatenate([to_senders, -to_receivers], axis=1)), axis=0
+    )
+    summed = dot(to_all, jnp.concatenate([hot_s, hot_r], axis=1), NT)
+    grads[...] = (summed[: 9 * 8] + summed[10 * 8 : 19 * 8]).reshape(9, 8, atoms)
     copies = []
     for d in others:
         copy = pltpu.make_async_remote_copy(

time: 24.7 us -> 24.5 us (level)
  no operation moved by 1% of the time
where the time goes in v5:
time: 24.5 us; the launch traced here: 24.3 us
  Pallas kernels  23.7 us (97%)
  between operations  0.65 us (3%)
    pallas_call x1, Pallas kernels, local(): pl.pallas_call(functools.partial(kernel, layers), out_shape=jax.ShapeDtyp...  22.3 us
    pallas_call x1, Pallas kernels, local(): pl.pallas_call(settle, out_shape=(jax.ShapeDtypeStruct(operands[0].shape,...  1.34 us

profile of v5, /device:TPU:1, one launch (start us, length us, event | category | flops | bytes accessed | tf_op | source)
XLA Modules:
  0.0 24.3 jit_solution(5621062267661807665)
XLA Ops:
  0.6 22.3 %shard_map.194.back_ref = f32[9,8,128]{2,1,0:T(8,128)} custom-call(f32[1,3,1,128]{3,2,1,0:T(1,128)} %bitcast.18, s32[1,1,128]{2,1,0:T(1,128)} %refs_1_.1, s32[1,3,1,128]{3,2,1,0:T(1,128)} %bitcast.19, s32[1,1,128]{2,1,0:T(1,128)} %refs_3_.1, s32[1,1,64]{2,1,0:T(1,128)} %refs_4_.1, s32[1,3,1,128]{3,2,1,0:T(1,128)} %bitcast.20, f32[5,128]{1,0:T(8,128)} %bitcast.15, ...), custom_call_target="tpu_custom_call" | custom-call | tf_op jit(solution)/shard_map/pallas_call | solution.py:470
  23.0 1.3 %shard_map.195 = (f32[1,3,1,128]{3,2,1,0:T(1,128)}, f32[1,1,128]{2,1,0:T(1,128)}) custom-call(f32[9,8,128]{2,1,0:T(8,128)} %shard_map.194.back_ref), custom_call_target="tpu_custom_call" | custom-call | tf_op jit(solution)/shard_map/pallas_call | solution.py:489

commit v6 on v5

--- a/solution.py
+++ b/solution.py
@@ -109,16 +109,16 @@
     return h * gate, gate * (1.0 + h * (1.0 - gate))
 
 
-def radial(basis, w_in, w_mid, w_out):
-    s1, g1 = silu_pair(mm(w_in, basis))
-    s2, g2 = silu_pair(mm(w_mid, s1))
-    return mm(w_out, s2), g1, g2
-
-
-def radial_back(g_out, w_in, w_mid, w_out, g1, g2):
-    gh2 = mm_rows(w_out, g_out) * g2
-    gh1 = mm(w_mid, gh2) * g1
-    return mm(w_in, gh1)
+def radial(nets):
+    first = [silu_pair(mm(w_in, basis)) for basis, w_in, _, _ in nets]
+    second = [silu_pair(mm(net[2], s[0])) for net, s in zip(nets, first)]
+    return [(mm(net[3], s[0]), f[1], s[1]) for net, f, s in zip(nets, first, second)]
+
+
+def radial_back(nets):
+    upper = [mm_rows(net[3], net[0]) * net[5] for net in nets]
+    lower = [mm(net[2], g) * net[4] for net, g in zip(nets, upper)]
+    return [mm(net[1], g) for net, g in zip(nets, lower)]
 
 
 def kernel(
@@ -219,7 +219,8 @@
     ro2_cols = jnp.broadcast_to(ro2_ref[...], (atoms, ro2_ref.shape[1])).T
 
     for copy in copies:
-        copy.wait()
+        copy.wait_recv()
+    sent_first = copies
 
     def tile(x):
         return jnp.concatenate([x] * slots, axis=1)
@@ -309,7 +310,9 @@
     hot_er = jnp.where(species_row == rec[3:4], 1.0, 0.0).astype(BF16)
     carrier = pick(emb, hot_es) * (live * (1.0 / slots))
     embedded = pick(emb, hot_er)
-    edge_one, one_g1, one_g2 = radial(basis, wi1, wm1, wo1)
+    (edge_one, one_g1, one_g2), (edge_two, two_g1, two_g2) = radial(
+        [(basis, wi1, wm1, wo1), (own(basis), wi2, wm2, wo2)]
+    )
     carried = [rows_of(edge_one, l) * carrier for l in range(3)]
     moments = []
     for m in range(9):
@@ -327,7 +330,6 @@
         features += [mixed[:, i * wide : (i + 1) * wide] for i in range(len(MEMBERS[l]))]
 
     live_two = own(live) * (1.0 / slots)
-    edge_two, two_g1, two_g2 = radial(own(basis), wi2, wm2, wo2)
     shapes_two = [None] + [own(s) for s in shapes[1:]]
     at_two, to_x2, to_y2 = own(atom_s), own(to_x), own(to_y)
     ax = floor_div(at_two, column)
@@ -357,14 +359,8 @@
     for k in range(1, slots):
         gathered = gathered + own_slot(scalar, k)
     hidden, hidden_slope = silu_pair(mm_rows(both, gathered) + mm_rows(rh, features[0][:, :atoms]))
-    energy_two = jnp.sum(ro2_cols * hidden, axis=0, keepdims=True)
-    energy_one = jnp.sum(ro1_cols * features[0][:, :atoms], axis=0, keepdims=True)
     owners = jnp.concatenate([own_ref[0, k].astype(F32) for k in range(slots)], axis=1)
     decay = PAIR * jnp.exp(-own(radius)) * owners * own(live)
-    pair = decay * own(envelope)
-    energy = energy_one + energy_two
-    for k in range(slots):
-        energy = energy + own_slot(pair, k)
     g_radius_pair = decay * (own(d_envelope) - own(envelope))
 
     g_hidden = ro2_cols * hidden_slope
@@ -379,7 +375,6 @@
     g_shapes_two = [
         jnp.sum(g_proj[DEGREE[m]] * rows_of(sent, m), axis=0, keepdims=True) for m in range(1, 9)
     ]
-    g_basis_two = radial_back(g_edge_two, wi2_back, wm2_back, wo2_back, two_g1, two_g2)
     g_stacked = put(split(g_sent), hot_two)
     g_features = [rows_of(g_stacked, m) for m in range(9)]
     g_features[0] = g_features[0] + jnp.concatenate(
@@ -403,8 +398,11 @@
             if m > 0:
                 g_shapes.append(jnp.sum(tiled * carried[l], axis=0, keepdims=True))
         g_edge_one.append(total * carrier)
-    g_basis = radial_back(
-        jnp.concatenate(g_edge_one, axis=0), wi1_back, wm1_back, wo1_back, one_g1, one_g2
+    g_basis, g_basis_two = radial_back(
+        [
+            (jnp.concatenate(g_edge_one, axis=0), wi1_back, wm1_back, wo1_back, one_g1, one_g2),
+            (g_edge_two, wi2_back, wm2_back, wo2_back, two_g1, two_g2),
+        ]
     )
 
     g_basis = g_basis + spread(g_basis_two)
@@ -438,11 +436,19 @@
         )
         copy.start()
         copies.append(copy)
+    energy_two = jnp.sum(ro2_cols * hidden, axis=0, keepdims=True)
+    energy_one = jnp.sum(ro1_cols * features[0][:, :atoms], axis=0, keepdims=True)
+    pair = decay * own(envelope)
+    energy = energy_one + energy_two
+    for k in range(slots):
+        energy = energy + own_slot(pair, k)
     grads[4, 3:4, :] = energy
     copy = pltpu.make_async_copy(grads.at[4], back.at[4], send_b.at[4])
     copy.start()
     for copy in copies + [copy]:
         copy.wait()
+    for copy in sent_first:
+        copy.wait_send()
 
 
 def settle(back_ref, force_ref, energy_ref):

time: 24.5 us -> 23.7 us (0.967)
  Pallas kernels: 23.7 us -> 22.9 us
    pallas_call x1, Pallas kernels: 22.3 us -> 21.5 us  [local(): pl.pallas_call(functools.partial(kernel, layers), out_shape=jax.ShapeDtyp...]
where the time goes in v6:
time: 23.7 us; the launch traced here: 23.5 us
  Pallas kernels  22.9 us (97%)
  between operations  0.65 us (3%)
    pallas_call x1, Pallas kernels, local(): pl.pallas_call(functools.partial(kernel, layers), out_shape=jax.ShapeDtyp...  21.5 us
    pallas_call x1, Pallas kernels, local(): pl.pallas_call(settle, out_shape=(jax.ShapeDtypeStruct(operands[0].shape,...  1.34 us

profile of v6, /device:TPU:1, one launch (start us, length us, event | category | flops | bytes accessed | tf_op | source)
XLA Modules:
  0.0 23.5 jit_solution(1705433186638535027)
XLA Ops:
  0.6 21.5 %shard_map.194.back_ref = f32[9,8,128]{2,1,0:T(8,128)} custom-call(f32[1,3,1,128]{3,2,1,0:T(1,128)} %bitcast.18, s32[1,1,128]{2,1,0:T(1,128)} %refs_1_.1, s32[1,3,1,128]{3,2,1,0:T(1,128)} %bitcast.19, s32[1,1,128]{2,1,0:T(1,128)} %refs_3_.1, s32[1,1,64]{2,1,0:T(1,128)} %refs_4_.1, s32[1,3,1,128]{3,2,1,0:T(1,128)} %bitcast.20, f32[5,128]{1,0:T(8,128)} %bitcast.15, ...), custom_call_target="tpu_custom_call" | custom-call | tf_op jit(solution)/shard_map/pallas_call | solution.py:476
  22.2 1.3 %shard_map.195 = (f32[1,3,1,128]{3,2,1,0:T(1,128)}, f32[1,1,128]{2,1,0:T(1,128)}) custom-call(f32[9,8,128]{2,1,0:T(8,128)} %shard_map.194.back_ref), custom_call_target="tpu_custom_call" | custom-call | tf_op jit(solution)/shard_map/pallas_call | solution.py:495

commit v7 on v6

--- a/solution.py
+++ b/solution.py
@@ -367,15 +367,15 @@
     g_refined = mm(rh_back, g_hidden)
     g_gathered = mm(both_back, g_hidden)
     t = jnp.concatenate([g_gathered] * slots, axis=1) * live_two
-    g_edge_two = jnp.concatenate([t * projected[l] for l in range(3)], axis=0)
     g_proj = [t * rows_of(edge_two, l) for l in range(3)]
     g_sent = jnp.concatenate(
         [g_proj[0]] + [g_proj[DEGREE[m]] * shapes_two[m] for m in range(1, 9)], axis=0
     )
+    g_stacked = put(split(g_sent), hot_two)
     g_shapes_two = [
         jnp.sum(g_proj[DEGREE[m]] * rows_of(sent, m), axis=0, keepdims=True) for m in range(1, 9)
     ]
-    g_stacked = put(split(g_sent), hot_two)
+    g_edge_two = jnp.concatenate([t * projected[l] for l in range(3)], axis=0)
     g_features = [rows_of(g_stacked, m) for m in range(9)]
     g_features[0] = g_features[0] + jnp.concatenate(
         [g_refined + ro1_cols, jnp.zeros((channels, wide - atoms), F32)], axis=1

time: 23.7 us -> 23.7 us (level)
  no operation moved by 1% of the time
where the time goes in v7:
time: 23.7 us; the launch traced here: 23.5 us
  Pallas kernels  22.9 us (97%)
  between operations  0.65 us (3%)
    pallas_call x1, Pallas kernels, local(): pl.pallas_call(functools.partial(kernel, layers), out_shape=jax.ShapeDtyp...  21.5 us
    pallas_call x1, Pallas kernels, local(): pl.pallas_call(settle, out_shape=(jax.ShapeDtypeStruct(operands[0].shape,...  1.34 us

profile of v7, /device:TPU:1, one launch (start us, length us, event | category | flops | bytes accessed | tf_op | source)
XLA Modules:
  0.0 23.5 jit_solution(8308424721936204290)
XLA Ops:
  0.6 21.5 %shard_map.194.back_ref = f32[9,8,128]{2,1,0:T(8,128)} custom-call(f32[1,3,1,128]{3,2,1,0:T(1,128)} %bitcast.18, s32[1,1,128]{2,1,0:T(1,128)} %refs_1_.1, s32[1,3,1,128]{3,2,1,0:T(1,128)} %bitcast.19, s32[1,1,128]{2,1,0:T(1,128)} %refs_3_.1, s32[1,1,64]{2,1,0:T(1,128)} %refs_4_.1, s32[1,3,1,128]{3,2,1,0:T(1,128)} %bitcast.20, f32[5,128]{1,0:T(8,128)} %bitcast.15, ...), custom_call_target="tpu_custom_call" | custom-call | tf_op jit(solution)/shard_map/pallas_call | solution.py:476
  22.2 1.3 %shard_map.195 = (f32[1,3,1,128]{3,2,1,0:T(1,128)}, f32[1,1,128]{2,1,0:T(1,128)}) custom-call(f32[9,8,128]{2,1,0:T(8,128)} %shard_map.194.back_ref), custom_call_target="tpu_custom_call" | custom-call | tf_op jit(solution)/shard_map/pallas_call | solution.py:495
